TPU v7x, 32 devices: a whole 2x2x4 slice. The times are simulated.
32 devices in a mesh: fft: 8 (over z, x), chan: 4 (over y, core).
Axes of the slice: x: 2, y: 2, z: 4, core: 2. Of those that a mesh axis runs over, the one named last changes fastest.
Arguments:
- visibilities: float32 [32, 2, 32, 128], P(('fft', 'chan')), may hold values from -6 to 6
- positions: float32 [32, 2, 32, 128], P(('fft', 'chan')), may hold values from 0 to 1
- cell_row: int32 [32, 32, 128], P(('fft', 'chan')), may hold values from 4 to 59
- cell_column: int32 [32, 32, 128], P(('fft', 'chan')), may hold values from 4 to 1019
- kernel_class: int32 [32, 32, 128], P(('fft', 'chan')), may hold values from 0 to 3
- send_counts: int32 [32, 32], P(('fft', 'chan')), may hold values from 96 to 128, as said below
- tile_lists: int32 [32, 8, 384], P(('fft', 'chan')), may hold values from 0 to 4095, as said below
- tile_counts: int32 [32, 8], P(('fft', 'chan')), may hold values from 192 to 384, as said below
- model_image: float32 [8, 128, 32768], P('chan', 'fft'), may hold values from -6 to 6
- threshold: float32 [8], P('chan'), may hold values from 0.5 to 3
Outputs:
- updated_model: float32 [8, 128, 32768], P('chan', 'fft')
- residuals: float32 [32, 2, 32, 128], P(('fft', 'chan'))
Inputs may be any that keep to these rules, and one draw needn't show every extreme that they name: `send_counts`: for each receiver some sender uses all 128 slots to it. `tile_lists`: entries below a list's count name slots p of sender s with p < send_counts[s, d] for the receiver d, and no slot is named twice among the entries below the counts of one receiver; other entries are arbitrary slot numbers. `tile_counts`: on every receiver one list has exactly 384 entries in use.
All inputs are finite; a program needn't handle non-finite values.
Results may differ from a plain program's by a relative error of at most 0.0003.
Values sent between devices are 32-bit elements; how exact they have to be, the bound alone decides.
A program may use at most 192 MiB of HBM per device.

v0:
```python
import math

import jax
import jax.numpy as jnp
from jax import lax
from jax.sharding import PartitionSpec as P

BU = 64


LOOP_GAIN = 0.7
EXACT_ARITHMETIC = lax.Precision.HIGHEST


def kernel_table(center_cell, fraction, class_index, length):
    grid_cells = jnp.arange(length, dtype=jnp.int32)
    distance = grid_cells[None, :] - center_cell[:, None]
    half_width = class_index + 1
    inside = jnp.abs(distance) <= half_width[:, None]
    spread = 0.6 * half_width.astype(jnp.float32)
    offset = distance.astype(jnp.float32) - fraction[:, None]
    shape_value = jnp.exp(-offset * offset / (2.0 * spread[:, None] * spread[:, None]))
    return jnp.where(inside, shape_value, jnp.zeros_like(shape_value))


def band_phases(band_rows, image_rows, grid_side):
    row_index = jnp.arange(band_rows, dtype=jnp.int32)
    image_index = jnp.arange(image_rows, dtype=jnp.int32)
    phase_index = (grid_side // 2 + row_index)[None, :] * image_index[:, None] % image_rows
    angle = -2.0 * math.pi / image_rows * phase_index.astype(jnp.float32)
    return (jnp.cos(angle), jnp.sin(angle))


def phase_table(row_count, column_count, modulus, direction):
    product = (
        jnp.arange(row_count, dtype=jnp.int32)[:, None]
        * jnp.arange(column_count, dtype=jnp.int32)[None, :]
        % modulus
    )
    angle = direction * 2.0 * math.pi / modulus * product.astype(jnp.float32)
    return (jnp.cos(angle), jnp.sin(angle))


def split_lengths(length):
    lead_len = 1 << (length.bit_length() - 1) // 2
    return (lead_len, length // lead_len)


def spectral(real_part, imag_part, direction):
    row_total, length = real_part.shape
    lead_len, tail_len = split_lengths(length)
    lead_cos, lead_sin = phase_table(lead_len, lead_len, lead_len, direction)
    twist_cos, twist_sin = phase_table(lead_len, tail_len, length, direction)
    trailing_cosine, trailing_sine = phase_table(tail_len, tail_len, tail_len, direction)
    split_re = real_part.reshape(row_total, lead_len, tail_len)
    step_re = jnp.einsum("kn,bnm->bkm", lead_cos, split_re, precision=EXACT_ARITHMETIC)
    step_im = jnp.einsum("kn,bnm->bkm", lead_sin, split_re, precision=EXACT_ARITHMETIC)
    split_im = imag_part.reshape(row_total, lead_len, tail_len)
    step_re = step_re - jnp.einsum("kn,bnm->bkm", lead_sin, split_im, precision=EXACT_ARITHMETIC)
    step_im = step_im + jnp.einsum("kn,bnm->bkm", lead_cos, split_im, precision=EXACT_ARITHMETIC)
    rotation_real = step_re * twist_cos - step_im * twist_sin
    rotation_imaginary = step_re * twist_sin + step_im * twist_cos
    folded_real = jnp.einsum(
        "nao,ov->nav", rotation_real, trailing_cosine, precision=EXACT_ARITHMETIC
    ) - jnp.einsum("nao,ov->nav", rotation_imaginary, trailing_sine, precision=EXACT_ARITHMETIC)
    return (folded_real, None)


def spectral_from_folded(folded, direction):
    row_total, lead_len, tail_len = folded.shape
    length = lead_len * tail_len
    tail_cos, tail_sin = phase_table(tail_len, tail_len, tail_len, direction)
    twist_cos, twist_sin = phase_table(lead_len, tail_len, length, direction)
    lead_cos, lead_sin = phase_table(lead_len, lead_len, lead_len, direction)
    first_re = jnp.einsum("bkv,vw->bkw", folded, tail_cos, precision=EXACT_ARITHMETIC)
    first_im = jnp.einsum("bkv,vw->bkw", folded, tail_sin, precision=EXACT_ARITHMETIC)
    turned_re = first_re * twist_cos - first_im * twist_sin
    turned_im = first_re * twist_sin + first_im * twist_cos
    out_re = jnp.einsum(
        "jk,bkw->bjw", lead_cos, turned_re, precision=EXACT_ARITHMETIC
    ) - jnp.einsum("jk,bkw->bjw", lead_sin, turned_im, precision=EXACT_ARITHMETIC)
    out_im = jnp.einsum(
        "jk,bkw->bjw", lead_sin, turned_re, precision=EXACT_ARITHMETIC
    ) + jnp.einsum("jk,bkw->bjw", lead_cos, turned_im, precision=EXACT_ARITHMETIC)
    return (out_re.reshape(row_total, length), out_im.reshape(row_total, length))


def to_rows(panel):
    return lax.all_to_all(panel, "fft", split_axis=2, concat_axis=3, tiled=True)


def to_columns(panel):
    return lax.all_to_all(panel, "fft", split_axis=3, concat_axis=2, tiled=True)


def per_device(
    visibilities,
    positions,
    cell_row,
    cell_column,
    kernel_class,
    send_counts,
    tile_lists,
    tile_counts,
    model_image,
    threshold,
):
    fft_devices = lax.axis_size("fft")
    chan_devices = lax.axis_size("chan")
    senders = fft_devices * chan_devices
    per_pair = visibilities.shape[3]
    local_tiles = tile_lists.shape[1]
    tile_cap = tile_lists.shape[2]
    chan_local = model_image.shape[0]
    tiles_each = local_tiles // chan_local
    grid_side = model_image.shape[2]
    facet_rows = model_image.shape[1] * fft_devices
    band_rows = BU
    tile_cols = grid_side // (fft_devices * tiles_each)
    columns = grid_side // fft_devices
    dirty_scale = 1.0 / math.sqrt(fft_devices * tiles_each * tile_cap)
    back_scale = 0.5 / math.sqrt(facet_rows * grid_side)
    slot_total = senders * per_pair
    entry_total = local_tiles * tile_cap
    payload = jnp.concatenate([visibilities, positions], axis=1)
    labels = jnp.stack([cell_row, cell_column, kernel_class], axis=1)
    got_vals, got_labels = (
        lax.all_to_all(payload, ("fft", "chan"), split_axis=2, concat_axis=0, tiled=True),
        lax.all_to_all(labels, ("fft", "chan"), split_axis=2, concat_axis=0, tiled=True),
    )
    got_vals = got_vals.reshape(senders, 4, per_pair)
    got_labels = got_labels.reshape(senders, 3, per_pair)
    value_table = got_vals.transpose(1, 0, 2).reshape(4, slot_total)
    label_table = got_labels.transpose(1, 0, 2).reshape(3, slot_total)
    slot_lists = tile_lists[0]
    flat_slots = slot_lists.reshape(-1)
    live_entry = jnp.arange(tile_cap, dtype=jnp.int32)[None, :] < tile_counts[0][:, None]
    listed = live_entry.astype(jnp.float32)
    picked = (
        jnp.take(value_table, flat_slots, axis=1)
        .reshape(4, local_tiles, tile_cap)
        .transpose(1, 0, 2)
    )
    picked_labels = (
        jnp.take(label_table, flat_slots, axis=1)
        .reshape(3, local_tiles, tile_cap)
        .transpose(1, 0, 2)
    )

    def tile_kernels(tile_vals, tile_labels):
        row_kernel = kernel_table(tile_labels[0], tile_vals[2], tile_labels[2], band_rows)
        column_kernel = kernel_table(tile_labels[1], tile_vals[3], tile_labels[2], tile_cols)
        return (row_kernel, column_kernel)

    def grid_tile(item):
        tile_vals, tile_labels, tile_live = item
        row_kernel, column_kernel = tile_kernels(tile_vals, tile_labels)
        weighted = row_kernel[None] * (tile_vals[:2] * tile_live[None])[:, :, None]
        return jnp.einsum("cku,kv->cuv", weighted, column_kernel, precision=EXACT_ARITHMETIC)

    tiles_grid = lax.map(grid_tile, (picked, picked_labels, listed))
    col_grid = tiles_grid.reshape(chan_local, tiles_each, 2, band_rows, tile_cols).transpose(
        2, 0, 3, 1, 4
    )
    col_grid = col_grid.reshape(2, chan_local, band_rows, columns)
    band_cos, band_sin = band_phases(band_rows, facet_rows, grid_side)
    band_re = jnp.einsum(
        "lu,cuv->clv", band_cos, col_grid[0], precision=EXACT_ARITHMETIC
    ) - jnp.einsum("lu,cuv->clv", band_sin, col_grid[1], precision=EXACT_ARITHMETIC)
    band_im = jnp.einsum(
        "lu,cuv->clv", band_cos, col_grid[1], precision=EXACT_ARITHMETIC
    ) + jnp.einsum("lu,cuv->clv", band_sin, col_grid[0], precision=EXACT_ARITHMETIC)
    image_rows = to_rows(jnp.stack([band_re, band_im]))
    row_local = model_image.shape[1]
    dirty_folded, unused_part = spectral(
        image_rows[0].reshape(-1, grid_side), image_rows[1].reshape(-1, grid_side), -1
    )
    lead_len, tail_len = split_lengths(grid_side)
    dirty_folded = dirty_folded.reshape(chan_local, row_local, lead_len, tail_len) * dirty_scale
    model_folded = model_image.reshape(chan_local, row_local, tail_len, lead_len).transpose(
        0, 1, 3, 2
    )
    folded_clip = threshold[:, None, None, None]
    updated_folded = model_folded + LOOP_GAIN * (
        dirty_folded - jnp.clip(dirty_folded, -folded_clip, folded_clip)
    )
    updated = updated_folded.transpose(0, 1, 3, 2).reshape(model_image.shape)
    inv_re, inv_im = spectral_from_folded(updated_folded.reshape(-1, lead_len, tail_len), 1)
    inverse = jnp.stack([inv_re, inv_im]).reshape(2, chan_local, row_local, grid_side)
    inv_cols = to_columns(inverse)
    pred_re = (
        jnp.einsum("lu,clv->cuv", band_cos, inv_cols[0], precision=EXACT_ARITHMETIC)
        + jnp.einsum("lu,clv->cuv", band_sin, inv_cols[1], precision=EXACT_ARITHMETIC)
    ) * back_scale
    pred_im = (
        jnp.einsum("lu,clv->cuv", band_cos, inv_cols[1], precision=EXACT_ARITHMETIC)
        - jnp.einsum("lu,clv->cuv", band_sin, inv_cols[0], precision=EXACT_ARITHMETIC)
    ) * back_scale
    pred_grid = jnp.stack([pred_re, pred_im])
    tile_pred = pred_grid.reshape(2, chan_local, band_rows, tiles_each, tile_cols).transpose(
        1, 3, 0, 2, 4
    )
    tile_pred = tile_pred.reshape(local_tiles, 2, band_rows, tile_cols)

    def degrid_tile(item):
        tile_vals, tile_labels, tile_live, tile_grid = item
        row_kernel, column_kernel = tile_kernels(tile_vals, tile_labels)
        partial_value = jnp.einsum("ku,cuv->ckv", row_kernel, tile_grid, precision=EXACT_ARITHMETIC)
        return jnp.sum(partial_value * column_kernel[None], axis=2) * tile_live[None]

    predicted = lax.map(degrid_tile, (picked, picked_labels, listed, tile_pred))
    entry_values = predicted.transpose(0, 2, 1).reshape(entry_total, 2)
    entry_values = jnp.concatenate([entry_values, jnp.zeros((1, 2), jnp.float32)], axis=0)
    target_slot = jnp.where(live_entry.reshape(-1), flat_slots, slot_total)
    owner = (
        jnp.full((slot_total,), entry_total, jnp.int32)
        .at[target_slot]
        .set(jnp.arange(entry_total, dtype=jnp.int32), mode="drop")
    )
    received = jnp.take(entry_values, owner, axis=0)
    outgoing = received.reshape(senders, per_pair, 2).transpose(0, 2, 1)[:, :, None, :]
    returned = lax.all_to_all(outgoing, ("fft", "chan"), split_axis=0, concat_axis=2, tiled=True)
    sent_live = jnp.arange(per_pair, dtype=jnp.int32)[None, None, :] < send_counts[0][None, :, None]
    residuals = jnp.where(sent_live[:, None], visibilities - returned, jnp.zeros_like(visibilities))
    return (updated, residuals)


def solution(mesh):
    placed = (
        P(("fft", "chan"), None, None, None),
        P(("fft", "chan"), None, None, None),
        P(("fft", "chan"), None, None),
        P(("fft", "chan"), None, None),
        P(("fft", "chan"), None, None),
        P(("fft", "chan"), None),
        P(("fft", "chan"), None, None),
        P(("fft", "chan"), None),
        P("chan", "fft", None),
        P("chan"),
    )
    return jax.shard_map(
        per_device,
        mesh=mesh,
        in_specs=placed,
        out_specs=(P("chan", "fft", None), P(("fft", "chan"), None, None, None)),
        check_vma=False,
    )
```

profile of v0, /device:TPU:0, one launch (start us, length us, event | category | flops | bytes accessed | tf_op | source)
XLA Modules:
  0.0 1206.9 jit_solution(11824001229612687900)
XLA Ops:
  2.0 7.3 all-to-all-start
  20.9 10.8 gather_fusion
  34.3 10.8 gather_fusion.1
  47.0 23.0 %while.24 = (s32[]{:T(128)}, f32[8,2,64,1024]{3,2,1,0:T(8,128)}, s32[8,3,384]{2,1,0:T(4,128)S(1)}, f32[8,4,384]{2,1,0:T(4,128)S(1)}, f32[8,384]{1,0:T(8,128)S(1)}, /*index=5*/s32[]{:T(128)}, s32[]{:T(128)}, s32[]{}, s32[]{}, s32[]{}) while((s32[]{:T(128)}, f32[8,2,64,1024]{3,2,1,0:T(8,128)}, s32[8,3,384]{2,1,0:T(4,128)S(1)}, ...), condition=%wide.region_1.2_spmd, body=%wide.region_0.1_spmd.sunk | while | flops 607791744 | bytes 766121 | solution.py:161
  70.1 4.9 copy.185
  84.6 6.9 fusion.147
  91.5 7.3 fusion.145
  98.7 6.9 fusion.67
  105.7 7.1 fusion.66
  116.6 13.3 %copy.140 = f32[2,2,128,4096]{3,1,0,2:T(2,128)} copy(f32[2,2,128,4096]{2,3,1,0:T(8,128)} %pad_maximum_fusion) | data formatting | bytes 16777216 | tf_op jit(solution)/shard_map/stack | solution.py:173
  129.8 5.8 all-to-all-start.2
  135.7 4.9 copy.180
  140.6 5.4 copy.131
  147.7 171.4 %all-to-all-done.2 = f32[2,2,128,4096]{3,1,0,2:T(2,128)} async-done(((f32[2,2,128,4096]{3,1,0,2:T(2,128)}), f32[2,2,128,4096]{3,1,0,2:T(2,128)}, u32[]{:S(2)}, u32[]{:S(2)}) %all-to-all-start.2) | async-done | bytes 8388640 | tf_op jit(solution)/shard_map/all_to_all | solution.py:89
  319.1 8.3 copy.141
  334.6 4.9 reshape_reshape_squeeze.6
  339.5 10.7 fusion.128
  350.2 8.6 fusion.124
  358.8 4.4 copy.144
  363.2 4.9 reshape_reshape_squeeze.7
  368.1 10.0 convolution_subtract_fusion.2
  378.1 7.1 convolution_add_fusion.2
  385.2 8.5 fusion.73
  393.8 8.4 subtract_multiply_fusion
  403.4 5.0 fusion.88
  408.5 4.5 fusion.90
  413.0 7.5 fusion.85
  420.6 8.6 fusion.84
  429.2 8.8 subtract_bitcast_fusion
  438.0 5.6 copy.155
  443.6 4.9 stack.44
  448.5 11.5 add_bitcast_fusion
  460.0 5.6 copy.158
  465.6 5.0 stack.45
  470.5 7.3 pad_maximum_fusion.1
  477.8 71.5 %copy.159 = f32[2,2,16,32768]{2,1,0,3:T(2,128)} copy(f32[2,2,16,32768]{3,2,1,0:T(8,128)} %pad_maximum_fusion.1) | data formatting | bytes 16777216 | tf_op jit(solution)/shard_map/stack | solution.py:189
  549.3 122.5 %reshape.607 = f32[8,1,262144]{2,1,0:T(1,128)} reshape(f32[32768,2,2,16]{3,2,1,0:T(2,128)} %bitcast.206) | data formatting | bytes 16777216
  671.8 5.0 all-to-all-start.3
  676.8 11.9 scatter_custom_fusion
  688.8 170.5 %all-to-all-done.3 = f32[8,1,262144]{2,1,0:T(1,128)} async-done(((f32[8,1,262144]{2,1,0:T(1,128)}), f32[8,1,262144]{2,1,0:T(1,128)}, u32[]{:S(2)}, u32[]{:S(2)}) %all-to-all-start.3) | async-done | bytes 8388640 | tf_op jit(solution)/shard_map/all_to_all | solution.py:93
  859.8 26.4 %reduce.24 = f32[8,262144]{1,0:T(8,128)} reduce(f32[8,1,262144]{2,1,0:T(1,128)} %all-to-all-done.3, f32[]{:T(128)} %broadcast.558), dimensions={1}, to_apply=%all_to_all.66.reduce_sub_computation | reduce | bytes 16777220 | tf_op jit(solution)/shard_map/all_to_all | solution.py:93
  886.2 137.6 %reshape.608 = f32[32768,2,2,16]{3,2,1,0:T(2,128)} reshape(f32[8,262144]{1,0:T(8,128)} %reduce.24) | data formatting | bytes 16777216
  1023.9 54.3 %copy.179 = f32[2,2,16,8,4096]{4,3,2,1,0:T(8,128)} copy(f32[2,2,16,8,4096]{2,1,0,4,3:T(2,128)} %bitcast.60) | data formatting | bytes 16777216 | tf_op jit(solution)/shard_map/all_to_all | solution.py:93
  1100.4 6.3 fusion.69
  1117.6 56.5 %while.25 = (s32[]{:T(128)}, f32[8,2,384]{2,1,0:T(2,128)S(1)}, f32[8,2,64,1024]{3,2,1,0:T(8,128)}, s32[8,3,384]{2,1,0:T(4,128)}, f32[8,4,384]{2,1,0:T(4,128)}, /...) while((s32[]{:T(128)}, f32[8,2,384]{2,1,0:T(2,128)S(1)}, ...), condition=%wide.region_5.6_spmd, body=%wide.region_3.5_spmd.sunk | while | flops 609314688 | bytes 3715761 | solution.py:211
  1174.7 14.1 %gather_fusion.2 = f32[4096,2]{1,0:T(8,128)} fusion(f32[3073,2]{1,0:T(8,128)S(1)} %concatenate.9, s32[4096]{0:T(1024)S(1)} %fusion.178), kind=kCustom, calls=%fused_computation.2 | custom fusion | bytes 81920 | tf_op jit(solution)/shard_map/jit(_take)/gather | solution.py:220
  1195.4 5.4 copy.150
  1200.8 4.9 reshape.544
  (208 shorter events, 161.2 us)
Async XLA Ops:
  2.0 14.6 %all-to-all-start = ((s32[1,3,32,128]{3,0,1,2:T(1,128)}), s32[1,3,32,128]{3,0,1,2:T(1,128)S(1)}, u32[]{:S(2)}, u32[]{:S(2)}) async-start(s32[1,3,32,128]{3,0,1,2:T(1,128)} %pad_add_fusion), calls=%async_computation | async-start | bytes 98304 | tf_op jit(solution)/shard_map/all_to_all | solution.py:129
  14.4 91.3 %copy-start.15 = (s32[64]{0:T(128)}, s32[64]{0:T(128)S(1)}, u32[]{:S(2)}) copy-start(s32[64]{0:T(128)S(1)} %iota_add_fusion) | copy-start | bytes 772
  16.7 17.0 %all-to-all-start.1 = ((f32[1,4,32,128]{3,1,0,2:T(4,128)}), f32[1,4,32,128]{3,1,0,2:T(4,128)S(1)}, u32[]{:S(2)}, u32[]{:S(2)}) async-start(f32[1,4,32,128]{3,1,0,2:T(4,128)} %pad_maximum_fusion.2), calls=%async_computation.1 | async-start | bytes 131072 | tf_op jit(solution)/shard_map/all_to_all | solution.py:128
  70.1 4.9 copy-start.11
  70.1 4.9 copy-start.12
  70.1 5.0 copy-start.14
  84.6 6.9 copy-start.6
  129.8 189.3 %all-to-all-start.2 = ((f32[2,2,128,4096]{3,1,0,2:T(2,128)}), f32[2,2,128,4096]{3,1,0,2:T(2,128)}, u32[]{:S(2)}, u32[]{:S(2)}) async-start(f32[2,2,128,4096]{3,1,0,2:T(2,128)} %copy.140), calls=%async_computation.2 | async-start | bytes 16777216 | tf_op jit(solution)/shard_map/all_to_all | solution.py:89
  140.6 5.4 copy-start.17
  339.5 10.7 copy-start.5
  350.2 8.6 copy-start.9
  368.1 10.0 copy-start.3
  368.1 10.0 copy-start.8
  393.8 8.4 copy-start.7
  403.4 5.0 copy-start.2
  408.5 20.7 %copy-start = (f32[32,128,256]{2,1,0:T(8,128)}, f32[32,128,256]{2,1,0:T(8,128)S(1)}, u32[]{:S(2)}) copy-start(f32[32,128,256]{2,1,0:T(8,128)S(1)} %fusion.88) | copy-start | bytes 12582916
  413.0 16.2 %copy-start.1 = (f32[32,128,256]{2,1,0:T(8,128)}, f32[32,128,256]{2,1,0:T(8,128)S(1)}, u32[]{:S(2)}) copy-start(f32[32,128,256]{2,1,0:T(8,128)S(1)} %fusion.90) | copy-start | bytes 12582916
  671.8 187.5 %all-to-all-start.3 = ((f32[8,1,262144]{2,1,0:T(1,128)}), f32[8,1,262144]{2,1,0:T(1,128)}, u32[]{:S(2)}, u32[]{:S(2)}) async-start(f32[8,1,262144]{2,1,0:T(1,128)} %reshape.607), calls=%async_computation.3 | async-start | bytes 16777216 | tf_op jit(solution)/shard_map/all_to_all | solution.py:93
  1082.1 2.5 copy-start.16
  1084.6 5.2 copy-start.4
  1106.7 3.8 copy-start.10
  1174.7 20.6 %copy-start.18 = (s32[1,32]{1,0:T(1,128)S(1)}, s32[1,32]{1,0:T(1,128)}, u32[]{:S(2)}) copy-start(s32[1,32]{1,0:T(1,128)} %param.19) | copy-start | bytes 388
  1191.7 14.1 %all-to-all-start.4 = ((f32[32,2,1,128]{3,1,2,0:T(2,128)}), f32[32,2,1,128]{3,1,2,0:T(2,128)S(1)}, u32[]{:S(2)}, u32[]{:S(2)}) async-start(f32[32,2,1,128]{3,1,2,0:T(2,128)} %select_bitcast_fusion.2), calls=%async_computation.4 | async-start | bytes 65536 | tf_op jit(solution)/shard_map/all_to_all | solution.py:222
  1200.8 5.0 copy-start.13
where the time goes:
time: 1220 us; the launch traced here: 1210 us
  local copies, waits for them, and re-layouts  578 us (47%)
  waiting for transfers between devices  344 us (28%)
  matrix products  196 us (16%)
  other arithmetic  61 us (5%)
  starting transfers between devices  25.3 us (2%)
    unnamed x46, local copies, waits for them, and re-layouts  268 us
    all_to_all x1, waiting for transfers between devices, to_rows(): return lax.all_to_all(panel, 'fft', split_axis=2, concat_axis=3, tiled=True)  171 us
    all_to_all x1, waiting for transfers between devices, to_columns(): return lax.all_to_all(panel, 'fft', split_axis=3, concat_axis=2, tiled=True)  171 us
    another operation x3, local copies, waits for them, and re-layouts, per_device(): jnp.stack([inv_re, inv_im]).reshape(2, chan_local, row_local, grid_side)  81.4 us
    all_to_all x2, local copies, waits for them, and re-layouts, to_columns(): return lax.all_to_all(panel, 'fft', split_axis=3, concat_axis=2, tiled=True)  54.8 us
    dot_general x8, matrix products, degrid_tile(): jnp.einsum('ku,cuv->ckv', row_kernel, tile_grid, precision=EXACT_ARITHMETIC)  31.3 us
    all_to_all x1, other arithmetic, to_columns(): return lax.all_to_all(panel, 'fft', split_axis=3, concat_axis=2, tiled=True)  26.4 us
  transfers between devices with their start and end apart: 5, of which 3 were waited for; matrix products, arithmetic and copies ran while one was open for 4% of the time, Pallas kernels for 0%

commit v1 on v0

v1 whole, which is shorter than its diff:
```python
import functools
import math

import jax
import jax.numpy as jnp
import ml_dtypes
import numpy as np
from jax import lax
from jax.experimental import pallas as pl
from jax.experimental.pallas import tpu as pltpu
from jax.sharding import PartitionSpec as P

BU = 64
LOOP_GAIN = 0.7
LANES = 128
GROUPS = 8
SPAN = GROUPS * LANES
REACH = 144
VMEM_BYTES = 56 * 1024 * 1024
F32 = jnp.float32
BF16 = jnp.bfloat16
NN = (((1,), (0,)), ((), ()))
NT = (((1,), (1,)), ((), ()))


def split_table(table):
    table = np.asarray(table, np.float32)
    high = table.astype(ml_dtypes.bfloat16)
    low = (table - high.astype(np.float32)).astype(ml_dtypes.bfloat16)
    return np.stack([high, low])


def split(value):
    high = value.astype(BF16)
    low = (value - high.astype(F32)).astype(BF16)
    return high, low


def dot(a, b, dims):
    return lax.dot_general(a, b, dims, preferred_element_type=F32)


def dot3(a, b, dims):
    return dot(a[0], b[0], dims) + (dot(a[0], b[1], dims) + dot(a[1], b[0], dims))


def unit(product, modulus):
    angle = 2.0 * np.pi / modulus * (product % modulus)
    return np.cos(angle), np.sin(angle)


def transform_tables(grid_side):
    lead = grid_side // LANES
    long_index, short_index = np.arange(lead), np.arange(LANES)
    cos1, sin1 = unit(long_index[:, None] * long_index[None, :], lead)
    cos2, sin2 = unit(short_index[:, None] * short_index[None, :], LANES)
    twist_cos, twist_sin = unit(long_index[:, None] * short_index[None, :], grid_side)
    first = np.block([[cos1, sin1], [-sin1, cos1]])
    second = np.concatenate([cos2, sin2], axis=1)
    third = np.concatenate([cos2, sin2], axis=0)
    last = np.block([[cos1, -sin1], [sin1, cos1]])
    return (
        split_table(first),
        split_table(second),
        split_table(third),
        split_table(last),
        np.stack([twist_cos, twist_sin]).astype(np.float32),
        np.stack([twist_cos.T, twist_sin.T]).astype(np.float32),
    )


def gather_kernel(senders, width, data_ref, slot_ref, live_ref, out_ref, table_ref):
    padded = table_ref.shape[1]
    data = data_ref[...]
    high = data.astype(BF16).astype(F32)
    rest = data - high
    middle = rest.astype(BF16).astype(F32)
    low = (rest - middle).astype(BF16).astype(F32)
    parts = [high, middle, low]
    if padded > 3 * senders:
        parts.append(jnp.zeros((padded - 3 * senders, data.shape[1]), F32))
    table_ref[...] = jnp.concatenate(parts, axis=0).T.astype(BF16)
    lists, _, cap = slot_ref.shape
    pieces = cap // width

    def step(index, carry):
        k = index // pieces
        at = pl.multiple_of(lax.rem(index, pieces) * width, LANES)
        slots = slot_ref[k, :, pl.ds(at, width)]
        live = live_ref[k, :, pl.ds(at, width)]
        source = slots // LANES
        place = slots - source * LANES
        sender = lax.broadcasted_iota(jnp.int32, (senders, width), 0)
        chosen = jnp.where(sender == source, 1.0, 0.0).astype(F32)
        picks = [chosen] * 3
        if padded > 3 * senders:
            picks.append(jnp.zeros((padded - 3 * senders, width), F32))
        picked = dot(table_ref[...], jnp.concatenate(picks, axis=0).astype(BF16), NN)
        here = lax.broadcasted_iota(jnp.int32, (LANES, width), 0) == place
        rows = []
        for part in range(7):
            block = picked[part * LANES : (part + 1) * LANES]
            rows.append(jnp.sum(jnp.where(here, block, 0.0), axis=0, keepdims=True))
        rows[0] = rows[0] * live
        rows[1] = rows[1] * live
        rows.append(live)
        out_ref[k, :, pl.ds(at, width)] = jnp.concatenate(rows, axis=0)
        return carry

    lax.fori_loop(0, lists * pieces, step, 0)


def scatter_kernel(senders, width, value_ref, slot_ref, live_ref, out_ref):
    lists, _, cap = slot_ref.shape
    pieces = cap // width
    out_ref[...] = jnp.zeros_like(out_ref)

    def step(index, carry):
        k = index // pieces
        at = pl.multiple_of(lax.rem(index, pieces) * width, LANES)
        slots = slot_ref[k, :, pl.ds(at, width)]
        live = live_ref[k, :, pl.ds(at, width)]
        values = value_ref[k, :, pl.ds(at, width)] * live
        source = slots // LANES
        place = slots - source * LANES
        sender = lax.broadcasted_iota(jnp.int32, (senders, width), 0)
        chosen = jnp.where(sender == source, 1.0, 0.0).astype(BF16)
        here = lax.broadcasted_iota(jnp.int32, (LANES, width), 0) == place
        spread = jnp.concatenate(
            [jnp.where(here, values[part : part + 1], 0.0) for part in range(2)], axis=0
        )
        high, low = split(spread)
        out_ref[...] += dot(chosen, high, NT) + dot(chosen, low, NT)
        return carry

    lax.fori_loop(0, lists * pieces, step, 0)


def cycle_kernel(
    plan,
    entry_ref,
    band_ref,
    model_ref,
    threshold_ref,
    first_ref,
    second_ref,
    third_ref,
    last_ref,
    twist_ref,
    twist_t_ref,
    updated_ref,
    predicted_ref,
    grid_ref,
    row_ref,
):
    (row_local, tiles_each, tile_cols, width, group, dirty_scale, back_scale) = plan
    owners, lists, _, cap = entry_ref.shape
    rows_total, lead2, _ = grid_ref.shape
    lead = lead2 // 2
    pieces = cap // width
    steps = owners * lists * pieces
    gathered = tile_cols < SPAN or pieces > 1

    def locate(index):
        piece = lax.rem(index, pieces)
        listing = index // pieces
        owner = listing // lists
        k = lax.rem(listing, lists)
        channel = k // tiles_each
        column = (owner * tiles_each + lax.rem(k, tiles_each)) * tile_cols
        span = column // SPAN
        inner = column - span * SPAN
        at = pl.multiple_of(piece * width, LANES)
        return owner, k, at, channel, span, inner

    def column_table(entries, inner):
        column = entries[5:6] + inner.astype(F32)
        half_width = entries[6:7] + 1.0
        rate = -1.0 / (0.72 * half_width * half_width)
        home = jnp.floor((column - 4.0) * (1.0 / LANES))
        local = column - home * LANES
        place = lax.broadcasted_iota(jnp.int32, (REACH, width), 0).astype(F32)
        distance = place - local
        offset = distance - entries[3:4]
        shape_value = jnp.exp(offset * offset * rate)
        table = jnp.where(jnp.abs(distance) <= half_width, shape_value, 0.0)
        high, low = split(table)
        rest = jnp.zeros((2 * LANES - REACH, width), BF16)
        high = jnp.concatenate([high, rest], axis=0)
        low = jnp.concatenate([low, rest], axis=0)
        which = lax.broadcasted_iota(jnp.int32, (GROUPS, width), 0).astype(F32)
        return (high, low), jnp.where(which == home, 1.0, 0.0)

    if gathered:
        grid_ref[...] = jnp.zeros_like(grid_ref)

    def grid_step(index, carry):
        owner, k, at, channel, span, inner = locate(index)
        entries = entry_ref[owner, k, :, pl.ds(at, width)]
        half_width = entries[6:7] + 1.0
        rate = -1.0 / (0.72 * half_width * half_width)
        band_row = lax.broadcasted_iota(jnp.int32, (BU, width), 0).astype(F32)
        distance = band_row - entries[4:5]
        offset = distance - entries[2:3]
        row_kernel = jnp.where(
            jnp.abs(distance) <= half_width, jnp.exp(offset * offset * rate), 0.0
        )
        phased = dot3((band_ref[0], band_ref[1]), split(row_kernel), NN)
        row_ref[index] = phased
        phased_re, phased_im = phased[:row_local], phased[row_local:]
        weight_re = entries[0:1] * phased_re - entries[1:2] * phased_im
        weight_im = entries[0:1] * phased_im + entries[1:2] * phased_re
        table, home = column_table(entries, inner)
        spread = jnp.concatenate(
            [
                jnp.broadcast_to(weight[i : i + 1], (GROUPS, width)) * home
                for weight in (weight_re, weight_im)
                for i in range(row_local)
            ],
            axis=0,
        )
        wide = dot3(split(spread), table, NT)
        block = wide[:, :LANES] + pltpu.roll(wide[:, LANES:], 1, 0)
        block = block.reshape(2, row_local, GROUPS, LANES)
        first_row = pl.multiple_of(channel * row_local, row_local)
        for part in range(2):
            spot = (
                pl.ds(first_row, row_local),
                pl.ds(pl.multiple_of(part * lead + span * GROUPS, GROUPS), GROUPS),
            )
            if gathered:
                grid_ref[spot] += block[part]
            else:
                grid_ref[spot] = block[part]
        return carry

    lax.fori_loop(0, steps, grid_step, 0)

    def image_step(index, carry):
        first_row = index * 2
        cos, sin = twist_ref[0], twist_ref[1]
        columns = jnp.concatenate([grid_ref[first_row], grid_ref[first_row + 1]], axis=1)
        stage = dot3((first_ref[0], first_ref[1]), split(columns), NN)
        cos_t, sin_t = twist_t_ref[0], twist_t_ref[1]
        turned_back = []
        for lane in range(2):
            row = first_row + lane
            real = stage[:lead, lane * LANES : (lane + 1) * LANES]
            imag = stage[lead:, lane * LANES : (lane + 1) * LANES]
            turned = jnp.concatenate([real * cos + imag * sin, imag * cos - real * sin], axis=1)
            dirty = dot3((second_ref[0], second_ref[1]), split(turned), NT) * dirty_scale
            level = threshold_ref[row // row_local]
            change = LOOP_GAIN * (dirty - jnp.clip(dirty, -level, level))
            halves = []
            for half in range(lead // LANES):
                spot = (
                    row // group,
                    pl.ds(half * group + lax.rem(row, group), LANES, stride=(lead // LANES) * group),
                )
                updated = model_ref[spot] + change[:, half * LANES : (half + 1) * LANES]
                updated_ref[spot] = updated
                halves.append(updated)
            image = jnp.concatenate(halves, axis=1)
            back = dot3((third_ref[0], third_ref[1]), split(image), NN)
            real, imag = back[:LANES], back[LANES:]
            turned_back.append(
                jnp.concatenate(
                    [real * cos_t - imag * sin_t, real * sin_t + imag * cos_t], axis=1
                )
            )
        columns = dot3(
            (last_ref[0], last_ref[1]), split(jnp.concatenate(turned_back, axis=0)), NT
        )
        grid_ref[first_row] = columns[:, :LANES]
        grid_ref[first_row + 1] = columns[:, LANES:]
        return carry

    lax.fori_loop(0, rows_total // 2, image_step, 0)

    def degrid_step(index, carry):
        owner, k, at, channel, span, inner = locate(index)
        entries = entry_ref[owner, k, :, pl.ds(at, width)]
        table, home = column_table(entries, inner)
        first_row = pl.multiple_of(channel * row_local, row_local)
        blocks = []
        for part in range(2):
            block = grid_ref[
                pl.ds(first_row, row_local),
                pl.ds(pl.multiple_of(part * lead + span * GROUPS, GROUPS), GROUPS),
            ]
            blocks.append(block.reshape(row_local * GROUPS, LANES))
        block = jnp.concatenate(blocks, axis=0)
        wide = jnp.concatenate([block, pltpu.roll(block, block.shape[0] - 1, 0)], axis=1)
        sampled = dot3(split(wide), table, NN)
        phased = row_ref[index]
        total_re = jnp.zeros((GROUPS, width), F32)
        total_im = jnp.zeros((GROUPS, width), F32)
        for i in range(row_local):
            real = sampled[i * GROUPS : (i + 1) * GROUPS]
            imag = sampled[(row_local + i) * GROUPS : (row_local + i + 1) * GROUPS]
            turn_re = phased[i : i + 1]
            turn_im = phased[row_local + i : row_local + i + 1]
            total_re += turn_re * real + turn_im * imag
            total_im += turn_re * imag - turn_im * real
        predicted_ref[owner, k, :, pl.ds(at, width)] = jnp.concatenate(
            [
                jnp.sum(total_re * home, axis=0, keepdims=True) * back_scale,
                jnp.sum(total_im * home, axis=0, keepdims=True) * back_scale,
            ],
            axis=0,
        )
        return carry

    lax.fori_loop(0, steps, degrid_step, 0)


def vmem(count):
    return [pl.BlockSpec(memory_space=pltpu.VMEM)] * count


def params():
    return pltpu.CompilerParams(vmem_limit_bytes=VMEM_BYTES)


def gather_entries(received, slots, live, width):
    senders = received.shape[0]
    padded = -(-3 * senders // LANES) * LANES
    lists, _, cap = slots.shape
    return pl.pallas_call(
        functools.partial(gather_kernel, senders, width),
        out_shape=jax.ShapeDtypeStruct((lists, 8, cap), F32),
        in_specs=vmem(3),
        out_specs=vmem(1)[0],
        scratch_shapes=[pltpu.VMEM((received.shape[1], padded), BF16)],
        compiler_params=params(),
        name="gather_entries",
    )(received, slots, live)


def scatter_values(values, slots, live, senders, width):
    return pl.pallas_call(
        functools.partial(scatter_kernel, senders, width),
        out_shape=jax.ShapeDtypeStruct((senders, 2 * LANES), F32),
        in_specs=vmem(3),
        out_specs=vmem(1)[0],
        compiler_params=params(),
        name="scatter_values",
    )(values, slots, live)


def imaging_cycle(entries, band, model, threshold, plan, grid_side):
    owners, lists, _, cap = entries.shape
    row_local, _, _, width, group = plan[:5]
    lead = grid_side // LANES
    rows_total = model.shape[0] * group
    steps = owners * lists * (cap // width)
    tables = transform_tables(grid_side)
    return pl.pallas_call(
        functools.partial(cycle_kernel, plan),
        out_shape=(
            jax.ShapeDtypeStruct(model.shape, F32),
            jax.ShapeDtypeStruct((owners, lists, 2, cap), F32),
        ),
        in_specs=vmem(3) + [pl.BlockSpec(memory_space=pltpu.SMEM)] + vmem(6),
        out_specs=tuple(vmem(2)),
        scratch_shapes=[
            pltpu.VMEM((rows_total, 2 * lead, LANES), F32),
            pltpu.VMEM((steps, 2 * row_local, width), F32),
        ],
        compiler_params=params(),
        name="imaging_cycle",
    )(entries, band, model, threshold, *[jnp.asarray(table) for table in tables])


def per_device(
    visibilities,
    positions,
    cell_row,
    cell_column,
    kernel_class,
    send_counts,
    tile_lists,
    tile_counts,
    model_image,
    threshold,
):
    fft_devices = lax.axis_size("fft")
    chan_devices = lax.axis_size("chan")
    senders = fft_devices * chan_devices
    per_pair = visibilities.shape[3]
    local_tiles = tile_lists.shape[1]
    tile_cap = tile_lists.shape[2]
    chan_local, row_local, grid_side = model_image.shape
    tiles_each = local_tiles // chan_local
    facet_rows = row_local * fft_devices
    tile_cols = grid_side // (fft_devices * tiles_each)
    dirty_scale = 1.0 / math.sqrt(fft_devices * tiles_each * tile_cap)
    back_scale = 0.5 / math.sqrt(facet_rows * grid_side)
    width = 384 if tile_cap % 384 == 0 else LANES
    group = math.gcd(row_local, 8)

    labels = jnp.stack([cell_row, cell_column, kernel_class], axis=1).astype(F32)
    payload = jnp.concatenate([visibilities, positions, labels], axis=1)[0]
    payload = payload.transpose(1, 0, 2).reshape(senders, 7 * per_pair)
    received = lax.all_to_all(payload, ("fft", "chan"), split_axis=0, concat_axis=0, tiled=True)
    slots = tile_lists[0][:, None, :]
    live = jnp.arange(tile_cap, dtype=jnp.int32)[None, :] < tile_counts[0][:, None]
    live = live.astype(F32)[:, None, :]
    entries = gather_entries(received, slots, live, width)
    entries = lax.all_gather(entries, "fft", axis=0, tiled=False)

    band_index = np.arange(facet_rows)[:, None] * (grid_side // 2 + np.arange(BU))[None, :]
    band_cos, band_sin = unit(band_index, facet_rows)
    band = np.stack([band_cos, -band_sin]).reshape(2, fft_devices, row_local, BU)
    band = split_table(band.transpose(1, 0, 2, 3).reshape(fft_devices, 2 * row_local, BU))
    band = lax.dynamic_index_in_dim(
        jnp.asarray(band), lax.axis_index("fft"), axis=1, keepdims=False
    )
    lanes_total = grid_side // LANES
    rows_total = chan_local * row_local
    model = model_image.reshape(rows_total // group, group, lanes_total, LANES)
    model = model.transpose(0, 2, 1, 3).reshape(rows_total // group, lanes_total * group, LANES)
    plan = (row_local, tiles_each, tile_cols, width, group, dirty_scale, back_scale)
    updated, partial = imaging_cycle(entries, band, model, threshold, plan, grid_side)
    updated = updated.reshape(rows_total // group, lanes_total, group, LANES)
    updated = updated.transpose(0, 2, 1, 3).reshape(model_image.shape)

    partial = lax.all_to_all(partial, "fft", split_axis=0, concat_axis=0, tiled=True)
    predicted = jnp.sum(partial, axis=0)
    outgoing = scatter_values(predicted, slots, live, senders, width)
    returned = lax.all_to_all(outgoing, ("fft", "chan"), split_axis=0, concat_axis=0, tiled=True)
    returned = returned.reshape(senders, 2, per_pair).transpose(1, 0, 2)[None]
    sent_live = jnp.arange(per_pair, dtype=jnp.int32)[None, None, :] < send_counts[0][None, :, None]
    residuals = jnp.where(sent_live[:, None], visibilities - returned, jnp.zeros_like(visibilities))
    return (updated, residuals)


def solution(mesh):
    placed = (
        P(("fft", "chan"), None, None, None),
        P(("fft", "chan"), None, None, None),
        P(("fft", "chan"), None, None),
        P(("fft", "chan"), None, None),
        P(("fft", "chan"), None, None),
        P(("fft", "chan"), None),
        P(("fft", "chan"), None, None),
        P(("fft", "chan"), None),
        P("chan", "fft", None),
        P("chan"),
    )
    return jax.shard_map(
        per_device,
        mesh=mesh,
        in_specs=placed,
        out_specs=(P("chan", "fft", None), P(("fft", "chan"), None, None, None)),
        check_vma=False,
    )
```

time: 1220 us -> 200 us (0.16); the launches traced: 1210 us -> 199 us
  local copies, waits for them, and re-layouts: 578 us -> 5.53 us
  waiting for transfers between devices: 344 us -> 11.2 us
  matrix products: 196 us -> 0 us
  Pallas kernels: 0 us -> 122 us
  other arithmetic: 61 us -> 4.24 us
  blocking collectives: 0 us -> 45.5 us
  starting transfers between devices: 25.3 us -> 9.82 us
    all_to_all x5 -> x2, waiting for transfers between devices: 344 us -> 11.2 us  [the longest x1 7.17 us: per_device(): lax.all_to_all(outgoing, ('fft', 'chan'), split_axis=0, concat_axis=0, ti...]
    unnamed x46 -> x5, local copies, waits for them, and re-layouts: 268 us -> 0.66 us
    dot_general x36 -> x0, matrix products: 196 us -> none  [the longest x8 31.3 us: degrid_tile(): jnp.einsum('ku,cuv->ckv', row_kernel, tile_grid, precision=EXACT_ARITHMETIC)]
    pallas_call x0 -> x3, Pallas kernels: none -> 122 us  [the longest x1 114 us: imaging_cycle(): pl.pallas_call(functools.partial(cycle_kernel, plan), out_shape=(jax.Shap...]
    another operation x8 -> x1, local copies, waits for them, and re-layouts: 112 us -> 1.31 us  [per_device(): slots = tile_lists[0][:, None, :]]
    all_to_all x3 -> x2, local copies, waits for them, and re-layouts: 63 us -> 2.16 us  [the longest x1 1.4 us: per_device(): lax.all_to_all(outgoing, ('fft', 'chan'), split_axis=0, concat_axis=0, ti...]
    gather x6 -> x0, local copies, waits for them, and re-layouts: 41.7 us -> none  [the longest x2 16.3 us: per_device(): received = jnp.take(entry_values, owner, axis=0)]
    all_gather x0 -> x1, blocking collectives: none -> 34.4 us  [per_device(): entries = lax.all_gather(entries, 'fft', axis=0, tiled=False)]
  transfers between devices with their start and end apart: 5 -> 2, of which waited for: 3 -> 2; matrix products, arithmetic and copies ran while one was open for 4% -> 2% of each run, Pallas kernels for 0% -> 0%
where the time goes in v1:
time: 200 us; the launch traced here: 199 us
  Pallas kernels  122 us (61%)
  blocking collectives  45.5 us (23%)
  waiting for transfers between devices  11.2 us (6%)
  starting transfers between devices  9.82 us (5%)
  local copies, waits for them, and re-layouts  5.53 us (3%)
  other arithmetic  4.24 us (2%)
    pallas_call x1, Pallas kernels, imaging_cycle(): pl.pallas_call(functools.partial(cycle_kernel, plan), out_shape=(jax.Shap...  114 us
    all_gather x1, blocking collectives, per_device(): entries = lax.all_gather(entries, 'fft', axis=0, tiled=False)  34.4 us
    all_to_all x1, blocking collectives, per_device(): lax.all_to_all(partial, 'fft', split_axis=0, concat_axis=0, tiled=True)  11.1 us
    all_to_all x1, starting transfers between devices, per_device(): lax.all_to_all(payload, ('fft', 'chan'), split_axis=0, concat_axis=0, til...  7.3 us
    all_to_all x1, waiting for transfers between devices, per_device(): lax.all_to_all(outgoing, ('fft', 'chan'), split_axis=0, concat_axis=0, ti...  7.17 us
    pallas_call x1, Pallas kernels, gather_entries(): pl.pallas_call(functools.partial(gather_kernel, senders, width), out_shap...  4.51 us
    all_to_all x1, waiting for transfers between devices, per_device(): lax.all_to_all(payload, ('fft', 'chan'), split_axis=0, concat_axis=0, til...  4.05 us
  transfers between devices with their start and end apart: 2, of which 2 were waited for; matrix products, arithmetic and copies ran while one was open for 2% of the time, Pallas kernels for 0%

profile of v1, /device:TPU:0, one launch (start us, length us, event | category | flops | bytes accessed | tf_op | source)
XLA Modules:
  0.0 199.4 jit_solution(8014192720461624845)
XLA Ops:
  0.6 0.8 add_convert_fusion
  1.4 0.8 maximum_bitcast_fusion
  2.2 0.1 copy.23
  2.3 0.8 all_to_all.22
  3.0 7.3 %all-to-all-start = ((f32[32,1,896]{2,1,0:T(1,128)}), f32[32,1,896]{2,1,0:T(1,128)S(1)}, u32[]{:S(2)}, u32[]{:S(2)}) async-start(f32[32,1,896]{2,1,0:T(1,128)} %all_to_all.22), calls=%async_computation | async-start | bytes 229376 | tf_op jit(solution)/shard_map/all_to_all | solution.py:405
  10.3 1.3 broadcast_in_dim_squeeze.2.slot_ref
  11.6 1.3 dynamic-slice_bitcast_fusion.band_ref
  13.0 1.3 compare_convert_fusion.live_ref
  14.3 4.0 %all-to-all-done = f32[32,1,896]{2,1,0:T(1,128)S(1)} async-done(((f32[32,1,896]{2,1,0:T(1,128)}), f32[32,1,896]{2,1,0:T(1,128)S(1)}, u32[]{:S(2)}, u32[]{:S(2)}) %all-to-all-start) | async-done | bytes 114720 | tf_op jit(solution)/shard_map/all_to_all | solution.py:405
  18.3 0.7 copy.30
  19.0 4.5 %gather_entries.1 = f32[8,8,384]{2,1,0:T(8,128)} custom-call(f32[32,896]{1,0:T(8,128)} %bitcast.35, s32[8,1,384]{2,1,0:T(1,128)} %broadcast_in_dim_squeeze.2.slot_ref, f32[8,1,384]{2,1,0:T(1,128)} %compare_convert_fusion.live_ref), custom_call_target="tpu_custom_call" | custom-call | tf_op jit(solution)/shard_map/gather_entries/pallas_call | solution.py:329
  23.5 34.4 %all-gather = f32[64,8,384]{2,1,0:T(8,128)} all-gather(f32[8,8,384]{2,1,0:T(8,128)} %gather_entries.1), channel_id=2, replica_groups=mesh['fft'=8,'chan'=4] {'fft'}, dimensions={0}, use_global_device_ids=true | all-gather | bytes 884736 | tf_op jit(solution)/shard_map/all_gather | solution.py:410
  57.9 0.0 copy-start.1
  57.9 0.0 copy-start
  57.9 114.5 %imaging_cycle.1 = (f32[4,2048,128]{2,1,0:T(8,128)}, f32[8,8,2,384]{3,2,1,0:T(2,128)}) custom-call(f32[8,8,8,384]{3,2,1,0:T(8,128)} %bitcast.34, bf16[2,32,64]{2,1,0:T(8,128)(2,1)} %dynamic-slice_bitcast_fusion.band_ref, f32[4,2048,128]{2,1,0:T(8,128)} %bitcast.33, f32[2]{0:T(128)} %threshold_ref.1, bf16[2,512,512]{2,1,0:T(8,128)(2,1)} %constant.30.clone.first_ref, ...), custom_call_target="tpu_custom_call" | custom-call | tf_op jit(solution)/shard_map/imaging_cycle/pallas_call | solution.py:358
  172.4 11.1 %all_to_all.26 = f32[8,8,2,384]{3,2,1,0:T(2,128)S(1)} all-to-all(f32[8,8,2,384]{3,2,1,0:T(2,128)} %get-tuple-element.5), channel_id=1, replica_groups=mesh['fft'=8,'chan'=4] {'fft'}, dimensions={0} | all-to-all | bytes 393216 | tf_op jit(solution)/shard_map/all_to_all | solution.py:428
  183.5 0.7 reduce_sum.9.value_ref
  184.2 3.5 %scatter_values.1 = f32[32,256]{1,0:T(8,128)} custom-call(f32[8,2,384]{2,1,0:T(2,128)} %reduce_sum.9.value_ref, s32[8,1,384]{2,1,0:T(1,128)} %broadcast_in_dim_squeeze.2.slot_ref, f32[8,1,384]{2,1,0:T(1,128)} %compare_convert_fusion.live_ref), custom_call_target="tpu_custom_call" | custom-call | tf_op jit(solution)/shard_map/scatter_values/pallas_call | solution.py:341
  187.6 1.4 copy.25
  189.0 2.5 %all-to-all-start.2 = ((f32[32,1,256]{2,1,0:T(1,128)}), f32[32,1,256]{2,1,0:T(1,128)S(1)}, u32[]{:S(2)}, u32[]{:S(2)}) async-start(f32[32,1,256]{2,1,0:T(1,128)} %copy.25), calls=%async_computation.2 | async-start | bytes 65536 | tf_op jit(solution)/shard_map/all_to_all | solution.py:431
  191.6 0.0 copy-done.1
  191.6 0.1 iota_compare_fusion
  191.7 7.2 %all-to-all-done.2 = f32[32,1,256]{2,1,0:T(1,128)S(1)} async-done(((f32[32,1,256]{2,1,0:T(1,128)}), f32[32,1,256]{2,1,0:T(1,128)S(1)}, u32[]{:S(2)}, u32[]{:S(2)}) %all-to-all-start.2) | async-done | bytes 32800 | tf_op jit(solution)/shard_map/all_to_all | solution.py:431
  198.8 0.0 copy-done
  198.8 0.6 fusion
Async XLA Ops:
  3.0 15.3 %all-to-all-start = ((f32[32,1,896]{2,1,0:T(1,128)}), f32[32,1,896]{2,1,0:T(1,128)S(1)}, u32[]{:S(2)}, u32[]{:S(2)}) async-start(f32[32,1,896]{2,1,0:T(1,128)} %all_to_all.22), calls=%async_computation | async-start | bytes 229376 | tf_op jit(solution)/shard_map/all_to_all | solution.py:405
  57.9 133.6 %copy-start.1 = (s32[1,32]{1,0:T(1,128)S(1)}, s32[1,32]{1,0:T(1,128)}, u32[]{:S(2)}) copy-start(s32[1,32]{1,0:T(1,128)} %param.22) | copy-start | bytes 388
  57.9 140.9 %copy-start = (f32[1,2,32,128]{3,2,1,0:T(8,128)S(1)}, f32[1,2,32,128]{3,2,1,0:T(8,128)}, u32[]{:S(2)}) copy-start(f32[1,2,32,128]{3,2,1,0:T(8,128)} %param.17) | copy-start | bytes 98308
  189.0 9.8 %all-to-all-start.2 = ((f32[32,1,256]{2,1,0:T(1,128)}), f32[32,1,256]{2,1,0:T(1,128)S(1)}, u32[]{:S(2)}, u32[]{:S(2)}) async-start(f32[32,1,256]{2,1,0:T(1,128)} %copy.25), calls=%async_computation.2 | async-start | bytes 65536 | tf_op jit(solution)/shard_map/all_to_all | solution.py:431

commit v2 on v1

--- a/solution.py
+++ b/solution.py
@@ -27,7 +27,12 @@
     table = np.asarray(table, np.float32)
     high = table.astype(ml_dtypes.bfloat16)
     low = (table - high.astype(np.float32)).astype(ml_dtypes.bfloat16)
-    return np.stack([high, low])
+    return high, low
+
+
+def table3(table):
+    high, low = split_table(table)
+    return np.concatenate([high, high, low], axis=-1)
 
 
 def split(value):
@@ -40,8 +45,9 @@
     return lax.dot_general(a, b, dims, preferred_element_type=F32)
 
 
-def dot3(a, b, dims):
-    return dot(a[0], b[0], dims) + (dot(a[0], b[1], dims) + dot(a[1], b[0], dims))
+def side3(value, axis):
+    high, low = split(value)
+    return jnp.concatenate([high, low, high], axis=axis)
 
 
 def unit(product, modulus):
@@ -60,10 +66,10 @@
     third = np.concatenate([cos2, sin2], axis=0)
     last = np.block([[cos1, -sin1], [sin1, cos1]])
     return (
-        split_table(first),
-        split_table(second),
-        split_table(third),
-        split_table(last),
+        table3(first),
+        table3(second),
+        table3(third),
+        table3(last),
         np.stack([twist_cos, twist_sin]).astype(np.float32),
         np.stack([twist_cos.T, twist_sin.T]).astype(np.float32),
     )
@@ -186,10 +192,8 @@
         table = jnp.where(jnp.abs(distance) <= half_width, shape_value, 0.0)
         high, low = split(table)
         rest = jnp.zeros((2 * LANES - REACH, width), BF16)
-        high = jnp.concatenate([high, rest], axis=0)
-        low = jnp.concatenate([low, rest], axis=0)
         which = lax.broadcasted_iota(jnp.int32, (GROUPS, width), 0).astype(F32)
-        return (high, low), jnp.where(which == home, 1.0, 0.0)
+        return high, low, rest, jnp.where(which == home, 1.0, 0.0)
 
     if gathered:
         grid_ref[...] = jnp.zeros_like(grid_ref)
@@ -205,12 +209,19 @@
         row_kernel = jnp.where(
             jnp.abs(distance) <= half_width, jnp.exp(offset * offset * rate), 0.0
         )
-        phased = dot3((band_ref[0], band_ref[1]), split(row_kernel), NN)
+        phased = dot(band_ref[...], side3(row_kernel, 0), NN)
         row_ref[index] = phased
         phased_re, phased_im = phased[:row_local], phased[row_local:]
         weight_re = entries[0:1] * phased_re - entries[1:2] * phased_im
         weight_im = entries[0:1] * phased_im + entries[1:2] * phased_re
-        table, home = column_table(entries, inner)
+        high, low, rest, home = column_table(entries, inner)
+        table = jnp.concatenate(
+            [
+                jnp.concatenate([high, low, high], axis=1),
+                jnp.concatenate([rest, rest, rest], axis=1),
+            ],
+            axis=0,
+        )
         spread = jnp.concatenate(
             [
                 jnp.broadcast_to(weight[i : i + 1], (GROUPS, width)) * home
@@ -219,7 +230,9 @@
             ],
             axis=0,
         )
-        wide = dot3(split(spread), table, NT)
+        spread_high, spread_low = split(spread)
+        spread = jnp.concatenate([spread_high, spread_high, spread_low], axis=1)
+        wide = dot(spread, table, NT)
         block = wide[:, :LANES] + pltpu.roll(wide[:, LANES:], 1, 0)
         block = block.reshape(2, row_local, GROUPS, LANES)
         first_row = pl.multiple_of(channel * row_local, row_local)
@@ -234,21 +247,25 @@
                 grid_ref[spot] = block[part]
         return carry
 
-    lax.fori_loop(0, steps, grid_step, 0)
+    lax.fori_loop(0, steps, grid_step, 0, unroll=2)
+
+    together = math.gcd(rows_total, 4)
 
     def image_step(index, carry):
-        first_row = index * 2
+        first_row = index * together
         cos, sin = twist_ref[0], twist_ref[1]
-        columns = jnp.concatenate([grid_ref[first_row], grid_ref[first_row + 1]], axis=1)
-        stage = dot3((first_ref[0], first_ref[1]), split(columns), NN)
         cos_t, sin_t = twist_t_ref[0], twist_t_ref[1]
+        columns = jnp.concatenate(
+            [grid_ref[first_row + lane] for lane in range(together)], axis=1
+        )
+        stage = dot(first_ref[...], side3(columns, 0), NN)
         turned_back = []
-        for lane in range(2):
+        for lane in range(together):
             row = first_row + lane
             real = stage[:lead, lane * LANES : (lane + 1) * LANES]
             imag = stage[lead:, lane * LANES : (lane + 1) * LANES]
             turned = jnp.concatenate([real * cos + imag * sin, imag * cos - real * sin], axis=1)
-            dirty = dot3((second_ref[0], second_ref[1]), split(turned), NT) * dirty_scale
+            dirty = dot(second_ref[...], side3(turned, 1), NT) * dirty_scale
             level = threshold_ref[row // row_local]
             change = LOOP_GAIN * (dirty - jnp.clip(dirty, -level, level))
             halves = []
@@ -261,26 +278,25 @@
                 updated_ref[spot] = updated
                 halves.append(updated)
             image = jnp.concatenate(halves, axis=1)
-            back = dot3((third_ref[0], third_ref[1]), split(image), NN)
+            back = dot(third_ref[...], side3(image, 0), NN)
             real, imag = back[:LANES], back[LANES:]
             turned_back.append(
                 jnp.concatenate(
                     [real * cos_t - imag * sin_t, real * sin_t + imag * cos_t], axis=1
                 )
             )
-        columns = dot3(
-            (last_ref[0], last_ref[1]), split(jnp.concatenate(turned_back, axis=0)), NT
-        )
-        grid_ref[first_row] = columns[:, :LANES]
-        grid_ref[first_row + 1] = columns[:, LANES:]
+        columns = dot(last_ref[...], side3(jnp.concatenate(turned_back, axis=0), 1), NT)
+        for lane in range(together):
+            grid_ref[first_row + lane] = columns[:, lane * LANES : (lane + 1) * LANES]
         return carry
 
-    lax.fori_loop(0, rows_total // 2, image_step, 0)
+    lax.fori_loop(0, rows_total // together, image_step, 0)
 
     def degrid_step(index, carry):
         owner, k, at, channel, span, inner = locate(index)
         entries = entry_ref[owner, k, :, pl.ds(at, width)]
-        table, home = column_table(entries, inner)
+        high, low, rest, home = column_table(entries, inner)
+        table = jnp.concatenate([high, rest, low, rest, high, rest], axis=0)
         first_row = pl.multiple_of(channel * row_local, row_local)
         blocks = []
         for part in range(2):
@@ -291,7 +307,8 @@
             blocks.append(block.reshape(row_local * GROUPS, LANES))
         block = jnp.concatenate(blocks, axis=0)
         wide = jnp.concatenate([block, pltpu.roll(block, block.shape[0] - 1, 0)], axis=1)
-        sampled = dot3(split(wide), table, NN)
+        wide_high, wide_low = split(wide)
+        sampled = dot(jnp.concatenate([wide_high, wide_high, wide_low], axis=1), table, NN)
         phased = row_ref[index]
         total_re = jnp.zeros((GROUPS, width), F32)
         total_im = jnp.zeros((GROUPS, width), F32)
@@ -311,7 +328,7 @@
         )
         return carry
 
-    lax.fori_loop(0, steps, degrid_step, 0)
+    lax.fori_loop(0, steps, degrid_step, 0, unroll=2)
 
 
 def vmem(count):
@@ -412,9 +429,9 @@
     band_index = np.arange(facet_rows)[:, None] * (grid_side // 2 + np.arange(BU))[None, :]
     band_cos, band_sin = unit(band_index, facet_rows)
     band = np.stack([band_cos, -band_sin]).reshape(2, fft_devices, row_local, BU)
-    band = split_table(band.transpose(1, 0, 2, 3).reshape(fft_devices, 2 * row_local, BU))
+    band = table3(band.transpose(1, 0, 2, 3).reshape(fft_devices, 2 * row_local, BU))
     band = lax.dynamic_index_in_dim(
-        jnp.asarray(band), lax.axis_index("fft"), axis=1, keepdims=False
+        jnp.asarray(band), lax.axis_index("fft"), axis=0, keepdims=False
     )
     lanes_total = grid_side // LANES
     rows_total = chan_local * row_local

time: 200 us -> 171 us (0.85)
  Pallas kernels: 122 us -> 93.4 us
    pallas_call x1, Pallas kernels: 114 us -> 85.4 us  [imaging_cycle(): pl.pallas_call(functools.partial(cycle_kernel, plan), out_shape=(jax.Shap...]
where the time goes in v2:
time: 171 us; the launch traced here: 170 us
  Pallas kernels  93.4 us (55%)
  blocking collectives  45.5 us (27%)
  waiting for transfers between devices  11.2 us (7%)
  starting transfers between devices  9.82 us (6%)
  local copies, waits for them, and re-layouts  5.53 us (3%)
  other arithmetic  4.24 us (2%)
    pallas_call x1, Pallas kernels, imaging_cycle(): pl.pallas_call(functools.partial(cycle_kernel, plan), out_shape=(jax.Shap...  85.4 us
    all_gather x1, blocking collectives, per_device(): entries = lax.all_gather(entries, 'fft', axis=0, tiled=False)  34.4 us
    all_to_all x1, blocking collectives, per_device(): lax.all_to_all(partial, 'fft', split_axis=0, concat_axis=0, tiled=True)  11.1 us
    all_to_all x1, starting transfers between devices, per_device(): lax.all_to_all(payload, ('fft', 'chan'), split_axis=0, concat_axis=0, til...  7.3 us
    all_to_all x1, waiting for transfers between devices, per_device(): lax.all_to_all(outgoing, ('fft', 'chan'), split_axis=0, concat_axis=0, ti...  7.17 us
    pallas_call x1, Pallas kernels, gather_entries(): pl.pallas_call(functools.partial(gather_kernel, senders, width), out_shap...  4.51 us
    all_to_all x1, waiting for transfers between devices, per_device(): lax.all_to_all(payload, ('fft', 'chan'), split_axis=0, concat_axis=0, til...  4.05 us
    pallas_call x1, Pallas kernels, scatter_values(): pl.pallas_call(functools.partial(scatter_kernel, senders, width), out_sha...  3.45 us
  transfers between devices with their start and end apart: 2, of which 2 were waited for; matrix products, arithmetic and copies ran while one was open for 2% of the time, Pallas kernels for 0%

profile of v2, /device:TPU:0, one launch (start us, length us, event | category | flops | bytes accessed | tf_op | source)
XLA Modules:
  0.0 170.4 jit_solution(6533833174110236999)
XLA Ops:
  0.6 0.8 add_convert_fusion
  1.4 0.8 maximum_bitcast_fusion
  2.2 0.1 copy.23
  2.3 0.8 all_to_all.22
  3.0 7.3 %all-to-all-start = ((f32[32,1,896]{2,1,0:T(1,128)}), f32[32,1,896]{2,1,0:T(1,128)S(1)}, u32[]{:S(2)}, u32[]{:S(2)}) async-start(f32[32,1,896]{2,1,0:T(1,128)} %all_to_all.22), calls=%async_computation | async-start | bytes 229376 | tf_op jit(solution)/shard_map/all_to_all | solution.py:422
  10.3 1.3 broadcast_in_dim_squeeze.2.slot_ref
  11.6 1.3 dynamic-slice_bitcast_fusion.band_ref
  13.0 1.3 compare_convert_fusion.live_ref
  14.3 4.0 %all-to-all-done = f32[32,1,896]{2,1,0:T(1,128)S(1)} async-done(((f32[32,1,896]{2,1,0:T(1,128)}), f32[32,1,896]{2,1,0:T(1,128)S(1)}, u32[]{:S(2)}, u32[]{:S(2)}) %all-to-all-start) | async-done | bytes 114720 | tf_op jit(solution)/shard_map/all_to_all | solution.py:422
  18.3 0.7 copy.30
  19.0 4.5 %gather_entries.1 = f32[8,8,384]{2,1,0:T(8,128)} custom-call(f32[32,896]{1,0:T(8,128)} %bitcast.35, s32[8,1,384]{2,1,0:T(1,128)} %broadcast_in_dim_squeeze.2.slot_ref, f32[8,1,384]{2,1,0:T(1,128)} %compare_convert_fusion.live_ref), custom_call_target="tpu_custom_call" | custom-call | tf_op jit(solution)/shard_map/gather_entries/pallas_call | solution.py:346
  23.5 34.4 %all-gather = f32[64,8,384]{2,1,0:T(8,128)} all-gather(f32[8,8,384]{2,1,0:T(8,128)} %gather_entries.1), channel_id=2, replica_groups=mesh['fft'=8,'chan'=4] {'fft'}, dimensions={0}, use_global_device_ids=true | all-gather | bytes 884736 | tf_op jit(solution)/shard_map/all_gather | solution.py:427
  57.9 0.0 copy-start.1
  57.9 0.0 copy-start
  57.9 85.4 %imaging_cycle.1 = (f32[4,2048,128]{2,1,0:T(8,128)}, f32[8,8,2,384]{3,2,1,0:T(2,128)}) custom-call(f32[8,8,8,384]{3,2,1,0:T(8,128)} %bitcast.34, bf16[32,192]{1,0:T(8,128)(2,1)} %dynamic-slice_bitcast_fusion.band_ref, f32[4,2048,128]{2,1,0:T(8,128)} %bitcast.33, f32[2]{0:T(128)} %threshold_ref.1, bf16[512,1536]{1,0:T(8,128)(2,1)} %constant.30.clone.first_ref, ...), custom_call_target="tpu_custom_call" | custom-call | tf_op jit(solution)/shard_map/imaging_cycle/pallas_call | solution.py:375
  143.3 11.1 %all_to_all.26 = f32[8,8,2,384]{3,2,1,0:T(2,128)S(1)} all-to-all(f32[8,8,2,384]{3,2,1,0:T(2,128)} %get-tuple-element.5), channel_id=1, replica_groups=mesh['fft'=8,'chan'=4] {'fft'}, dimensions={0} | all-to-all | bytes 393216 | tf_op jit(solution)/shard_map/all_to_all | solution.py:445
  154.4 0.7 reduce_sum.9.value_ref
  155.1 3.5 %scatter_values.1 = f32[32,256]{1,0:T(8,128)} custom-call(f32[8,2,384]{2,1,0:T(2,128)} %reduce_sum.9.value_ref, s32[8,1,384]{2,1,0:T(1,128)} %broadcast_in_dim_squeeze.2.slot_ref, f32[8,1,384]{2,1,0:T(1,128)} %compare_convert_fusion.live_ref), custom_call_target="tpu_custom_call" | custom-call | tf_op jit(solution)/shard_map/scatter_values/pallas_call | solution.py:358
  158.6 1.4 copy.25
  160.0 2.5 %all-to-all-start.2 = ((f32[32,1,256]{2,1,0:T(1,128)}), f32[32,1,256]{2,1,0:T(1,128)S(1)}, u32[]{:S(2)}, u32[]{:S(2)}) async-start(f32[32,1,256]{2,1,0:T(1,128)} %copy.25), calls=%async_computation.2 | async-start | bytes 65536 | tf_op jit(solution)/shard_map/all_to_all | solution.py:448
  162.5 0.0 copy-done.1
  162.5 0.1 iota_compare_fusion
  162.6 7.2 %all-to-all-done.2 = f32[32,1,256]{2,1,0:T(1,128)S(1)} async-done(((f32[32,1,256]{2,1,0:T(1,128)}), f32[32,1,256]{2,1,0:T(1,128)S(1)}, u32[]{:S(2)}, u32[]{:S(2)}) %all-to-all-start.2) | async-done | bytes 32800 | tf_op jit(solution)/shard_map/all_to_all | solution.py:448
  169.7 0.0 copy-done
  169.7 0.6 fusion
Async XLA Ops:
  3.0 15.3 %all-to-all-start = ((f32[32,1,896]{2,1,0:T(1,128)}), f32[32,1,896]{2,1,0:T(1,128)S(1)}, u32[]{:S(2)}, u32[]{:S(2)}) async-start(f32[32,1,896]{2,1,0:T(1,128)} %all_to_all.22), calls=%async_computation | async-start | bytes 229376 | tf_op jit(solution)/shard_map/all_to_all | solution.py:422
  57.9 104.6 %copy-start.1 = (s32[1,32]{1,0:T(1,128)S(1)}, s32[1,32]{1,0:T(1,128)}, u32[]{:S(2)}) copy-start(s32[1,32]{1,0:T(1,128)} %param.22) | copy-start | bytes 388
  57.9 111.8 %copy-start = (f32[1,2,32,128]{3,2,1,0:T(8,128)S(1)}, f32[1,2,32,128]{3,2,1,0:T(8,128)}, u32[]{:S(2)}) copy-start(f32[1,2,32,128]{3,2,1,0:T(8,128)} %param.17) | copy-start | bytes 98308
  160.0 9.8 %all-to-all-start.2 = ((f32[32,1,256]{2,1,0:T(1,128)}), f32[32,1,256]{2,1,0:T(1,128)S(1)}, u32[]{:S(2)}, u32[]{:S(2)}) async-start(f32[32,1,256]{2,1,0:T(1,128)} %copy.25), calls=%async_computation.2 | async-start | bytes 65536 | tf_op jit(solution)/shard_map/all_to_all | solution.py:448

commit v3 on v2

--- a/solution.py
+++ b/solution.py
@@ -75,21 +75,129 @@
     )
 
 
-def gather_kernel(senders, width, data_ref, slot_ref, live_ref, out_ref, table_ref):
+def cycle_kernel(
+    plan,
+    payload_ref,
+    slot_ref,
+    live_ref,
+    count_ref,
+    band_ref,
+    threshold_ref,
+    second_ref,
+    third_ref,
+    twist_ref,
+    twist_t_ref,
+    first_any,
+    last_any,
+    model_any,
+    updated_any,
+    residual_ref,
+    received_ref,
+    table_ref,
+    entry_ref,
+    first_ref,
+    last_ref,
+    model_ref,
+    updated_ref,
+    grid_ref,
+    row_ref,
+    predicted_ref,
+    arrived_ref,
+    outgoing_ref,
+    returned_ref,
+    load_sem,
+    payload_send,
+    payload_recv,
+    entry_send,
+    entry_recv,
+    partial_send,
+    partial_recv,
+    return_send,
+    return_recv,
+):
+    (chan_devices, row_local, tiles_each, tile_cols, width, group, dirty_scale, back_scale) = plan
+    owners, lists, _, cap = entry_ref.shape
+    senders = owners * chan_devices
+    rows_total, lead2, _ = grid_ref.shape
+    lead = lead2 // 2
+    pieces = cap // width
+    rounds = lists * pieces
+    gathered = tile_cols < SPAN or pieces > 1
+    fft_at, chan_at = lax.axis_index("fft"), lax.axis_index("chan")
+    me = fft_at * chan_devices + chan_at
+
+    def place_of(device):
+        return (device // chan_devices, lax.rem(device, chan_devices))
+
+    def send(source, target, send_sem, recv_sem, device):
+        return pltpu.make_async_remote_copy(
+            src_ref=source,
+            dst_ref=target,
+            send_sem=send_sem,
+            recv_sem=recv_sem,
+            device_id=device,
+            device_id_type=pl.DeviceIdType.MESH,
+        )
+
+    loads = [
+        pltpu.make_async_copy(source, target, load_sem.at[i])
+        for i, (source, target) in enumerate(
+            ((model_any, model_ref), (first_any, first_ref), (last_any, last_ref))
+        )
+    ]
+    for load in loads:
+        load.start()
+
+    barrier = pltpu.get_barrier_semaphore()
+    for ahead in range(1, senders):
+        pl.semaphore_signal(
+            barrier,
+            inc=1,
+            device_id=place_of(lax.rem(me + ahead, senders)),
+            device_id_type=pl.DeviceIdType.MESH,
+        )
+    pl.semaphore_wait(barrier, senders - 1)
+
+    def payload_copy(ahead):
+        target = lax.rem(me + ahead, senders)
+        return send(
+            payload_ref.at[target],
+            received_ref.at[me],
+            payload_send.at[ahead],
+            payload_recv.at[ahead],
+            place_of(target),
+        )
+
+    def payload_arrival(ahead):
+        source = lax.rem(me + senders - ahead, senders)
+        return send(
+            payload_ref.at[source],
+            received_ref.at[source],
+            payload_send.at[ahead],
+            payload_recv.at[ahead],
+            place_of(source),
+        )
+
+    for ahead in range(1, senders):
+        payload_copy(ahead).start()
+    received_ref[me] = payload_ref[me]
+    for ahead in range(1, senders):
+        payload_arrival(ahead).wait_recv()
+
     padded = table_ref.shape[1]
-    data = data_ref[...]
-    high = data.astype(BF16).astype(F32)
-    rest = data - high
-    middle = rest.astype(BF16).astype(F32)
-    low = (rest - middle).astype(BF16).astype(F32)
-    parts = [high, middle, low]
-    if padded > 3 * senders:
-        parts.append(jnp.zeros((padded - 3 * senders, data.shape[1]), F32))
-    table_ref[...] = jnp.concatenate(parts, axis=0).T.astype(BF16)
-    lists, _, cap = slot_ref.shape
-    pieces = cap // width
-
-    def step(index, carry):
+    for part in range(7):
+        data = received_ref[:, part, :]
+        high = data.astype(BF16).astype(F32)
+        rest = data - high
+        middle = rest.astype(BF16).astype(F32)
+        parts = [high, middle, rest - middle]
+        if padded > 3 * senders:
+            parts.append(jnp.zeros((padded - 3 * senders, LANES), F32))
+        table_ref[part * LANES : (part + 1) * LANES, :] = (
+            jnp.concatenate(parts, axis=0).T.astype(BF16)
+        )
+
+    def slots_of(index):
         k = index // pieces
         at = pl.multiple_of(lax.rem(index, pieces) * width, LANES)
         slots = slot_ref[k, :, pl.ds(at, width)]
@@ -98,11 +206,15 @@
         place = slots - source * LANES
         sender = lax.broadcasted_iota(jnp.int32, (senders, width), 0)
         chosen = jnp.where(sender == source, 1.0, 0.0).astype(F32)
+        here = lax.broadcasted_iota(jnp.int32, (LANES, width), 0) == place
+        return k, at, live, chosen, here
+
+    def pick_step(index, carry):
+        k, at, live, chosen, here = slots_of(index)
         picks = [chosen] * 3
         if padded > 3 * senders:
             picks.append(jnp.zeros((padded - 3 * senders, width), F32))
         picked = dot(table_ref[...], jnp.concatenate(picks, axis=0).astype(BF16), NN)
-        here = lax.broadcasted_iota(jnp.int32, (LANES, width), 0) == place
         rows = []
         for part in range(7):
             block = picked[part * LANES : (part + 1) * LANES]
@@ -110,74 +222,42 @@
         rows[0] = rows[0] * live
         rows[1] = rows[1] * live
         rows.append(live)
-        out_ref[k, :, pl.ds(at, width)] = jnp.concatenate(rows, axis=0)
+        entry_ref[fft_at, k, :, pl.ds(at, width)] = jnp.concatenate(rows, axis=0)
         return carry
 
-    lax.fori_loop(0, lists * pieces, step, 0)
-
-
-def scatter_kernel(senders, width, value_ref, slot_ref, live_ref, out_ref):
-    lists, _, cap = slot_ref.shape
-    pieces = cap // width
-    out_ref[...] = jnp.zeros_like(out_ref)
-
-    def step(index, carry):
+    lax.fori_loop(0, rounds, pick_step, 0, unroll=2)
+
+    def entry_copy(ahead):
+        return send(
+            entry_ref.at[fft_at],
+            entry_ref.at[fft_at],
+            entry_send.at[ahead],
+            entry_recv.at[ahead],
+            (lax.rem(fft_at + ahead, owners), chan_at),
+        )
+
+    def entry_arrival(ahead):
+        owner = lax.rem(fft_at + owners - ahead, owners)
+        return send(
+            entry_ref.at[owner],
+            entry_ref.at[owner],
+            entry_send.at[ahead],
+            entry_recv.at[ahead],
+            (owner, chan_at),
+        )
+
+    for ahead in range(1, owners):
+        entry_copy(ahead).start()
+
+    def locate(owner, index):
+        piece = lax.rem(index, pieces)
         k = index // pieces
-        at = pl.multiple_of(lax.rem(index, pieces) * width, LANES)
-        slots = slot_ref[k, :, pl.ds(at, width)]
-        live = live_ref[k, :, pl.ds(at, width)]
-        values = value_ref[k, :, pl.ds(at, width)] * live
-        source = slots // LANES
-        place = slots - source * LANES
-        sender = lax.broadcasted_iota(jnp.int32, (senders, width), 0)
-        chosen = jnp.where(sender == source, 1.0, 0.0).astype(BF16)
-        here = lax.broadcasted_iota(jnp.int32, (LANES, width), 0) == place
-        spread = jnp.concatenate(
-            [jnp.where(here, values[part : part + 1], 0.0) for part in range(2)], axis=0
-        )
-        high, low = split(spread)
-        out_ref[...] += dot(chosen, high, NT) + dot(chosen, low, NT)
-        return carry
-
-    lax.fori_loop(0, lists * pieces, step, 0)
-
-
-def cycle_kernel(
-    plan,
-    entry_ref,
-    band_ref,
-    model_ref,
-    threshold_ref,
-    first_ref,
-    second_ref,
-    third_ref,
-    last_ref,
-    twist_ref,
-    twist_t_ref,
-    updated_ref,
-    predicted_ref,
-    grid_ref,
-    row_ref,
-):
-    (row_local, tiles_each, tile_cols, width, group, dirty_scale, back_scale) = plan
-    owners, lists, _, cap = entry_ref.shape
-    rows_total, lead2, _ = grid_ref.shape
-    lead = lead2 // 2
-    pieces = cap // width
-    steps = owners * lists * pieces
-    gathered = tile_cols < SPAN or pieces > 1
-
-    def locate(index):
-        piece = lax.rem(index, pieces)
-        listing = index // pieces
-        owner = listing // lists
-        k = lax.rem(listing, lists)
         channel = k // tiles_each
         column = (owner * tiles_each + lax.rem(k, tiles_each)) * tile_cols
         span = column // SPAN
         inner = column - span * SPAN
         at = pl.multiple_of(piece * width, LANES)
-        return owner, k, at, channel, span, inner
+        return k, at, channel, span, inner
 
     def column_table(entries, inner):
         column = entries[5:6] + inner.astype(F32)
@@ -198,8 +278,8 @@
     if gathered:
         grid_ref[...] = jnp.zeros_like(grid_ref)
 
-    def grid_step(index, carry):
-        owner, k, at, channel, span, inner = locate(index)
+    def grid_step(owner, index):
+        k, at, channel, span, inner = locate(owner, index)
         entries = entry_ref[owner, k, :, pl.ds(at, width)]
         half_width = entries[6:7] + 1.0
         rate = -1.0 / (0.72 * half_width * half_width)
@@ -210,7 +290,7 @@
             jnp.abs(distance) <= half_width, jnp.exp(offset * offset * rate), 0.0
         )
         phased = dot(band_ref[...], side3(row_kernel, 0), NN)
-        row_ref[index] = phased
+        row_ref[owner * rounds + index] = phased
         phased_re, phased_im = phased[:row_local], phased[row_local:]
         weight_re = entries[0:1] * phased_re - entries[1:2] * phased_im
         weight_im = entries[0:1] * phased_im + entries[1:2] * phased_re
@@ -245,9 +325,24 @@
                 grid_ref[spot] += block[part]
             else:
                 grid_ref[spot] = block[part]
+
+    def grid_owner(ahead, carry):
+        owner = lax.rem(fft_at + owners - ahead, owners)
+
+        @pl.when(ahead > 0)
+        def _():
+            entry_arrival(ahead).wait_recv()
+
+        def step(index, inner_carry):
+            grid_step(owner, index)
+            return inner_carry
+
+        lax.fori_loop(0, rounds, step, 0, unroll=2)
         return carry
 
-    lax.fori_loop(0, steps, grid_step, 0, unroll=2)
+    lax.fori_loop(0, owners, grid_owner, 0)
+    for load in loads:
+        load.wait()
 
     together = math.gcd(rows_total, 4)
 
@@ -291,9 +386,11 @@
         return carry
 
     lax.fori_loop(0, rows_total // together, image_step, 0)
-
-    def degrid_step(index, carry):
-        owner, k, at, channel, span, inner = locate(index)
+    store = pltpu.make_async_copy(updated_ref, updated_any, load_sem.at[3])
+    store.start()
+
+    def degrid_step(owner, index):
+        k, at, channel, span, inner = locate(owner, index)
         entries = entry_ref[owner, k, :, pl.ds(at, width)]
         high, low, rest, home = column_table(entries, inner)
         table = jnp.concatenate([high, rest, low, rest, high, rest], axis=0)
@@ -309,7 +406,7 @@
         wide = jnp.concatenate([block, pltpu.roll(block, block.shape[0] - 1, 0)], axis=1)
         wide_high, wide_low = split(wide)
         sampled = dot(jnp.concatenate([wide_high, wide_high, wide_low], axis=1), table, NN)
-        phased = row_ref[index]
+        phased = row_ref[owner * rounds + index]
         total_re = jnp.zeros((GROUPS, width), F32)
         total_im = jnp.zeros((GROUPS, width), F32)
         for i in range(row_local):
@@ -326,67 +423,150 @@
             ],
             axis=0,
         )
+
+    def partial_copy(ahead):
+        owner = lax.rem(fft_at + ahead, owners)
+        return send(
+            predicted_ref.at[owner],
+            arrived_ref.at[ahead],
+            partial_send.at[ahead],
+            partial_recv.at[ahead],
+            (owner, chan_at),
+        )
+
+    def degrid_owner(turn, carry):
+        ahead = owners - 1 - turn
+        owner = lax.rem(fft_at + ahead, owners)
+
+        def step(index, inner_carry):
+            degrid_step(owner, index)
+            return inner_carry
+
+        lax.fori_loop(0, rounds, step, 0, unroll=2)
+
+        @pl.when(ahead > 0)
+        def _():
+            partial_copy(ahead).start()
+
         return carry
 
-    lax.fori_loop(0, steps, degrid_step, 0, unroll=2)
-
-
-def vmem(count):
-    return [pl.BlockSpec(memory_space=pltpu.VMEM)] * count
-
-
-def params():
-    return pltpu.CompilerParams(vmem_limit_bytes=VMEM_BYTES)
-
-
-def gather_entries(received, slots, live, width):
-    senders = received.shape[0]
-    padded = -(-3 * senders // LANES) * LANES
+    lax.fori_loop(0, owners, degrid_owner, 0)
+    for ahead in range(1, owners):
+        partial_copy(ahead).wait_recv()
+
+    def place_step(index, carry):
+        k, at, live, chosen, here = slots_of(index)
+        values = predicted_ref[fft_at, k, :, pl.ds(at, width)]
+        for ahead in range(1, owners):
+            values = values + arrived_ref[ahead, k, :, pl.ds(at, width)]
+        values = values * live
+        spread = jnp.concatenate(
+            [jnp.where(here, values[part : part + 1], 0.0) for part in range(2)], axis=0
+        )
+        high, low = split(spread)
+        chosen = chosen.astype(BF16)
+        return carry + (dot(chosen, high, NT) + dot(chosen, low, NT))
+
+    placed = lax.fori_loop(
+        0, rounds, place_step, jnp.zeros((senders, 2 * LANES), F32), unroll=2
+    )
+    for part in range(2):
+        outgoing_ref[:, part, :] = placed[:, part * LANES : (part + 1) * LANES]
+
+    def return_copy(ahead):
+        target = lax.rem(me + ahead, senders)
+        return send(
+            outgoing_ref.at[target],
+            returned_ref.at[me],
+            return_send.at[ahead],
+            return_recv.at[ahead],
+            place_of(target),
+        )
+
+    def return_arrival(ahead):
+        source = lax.rem(me + senders - ahead, senders)
+        return send(
+            outgoing_ref.at[source],
+            returned_ref.at[source],
+            return_send.at[ahead],
+            return_recv.at[ahead],
+            place_of(source),
+        )
+
+    for ahead in range(1, senders):
+        return_copy(ahead).start()
+    returned_ref[me] = outgoing_ref[me]
+    for ahead in range(1, senders):
+        return_arrival(ahead).wait_recv()
+    in_use = lax.broadcasted_iota(jnp.int32, (senders, LANES), 1) < count_ref[...]
+    for part in range(2):
+        difference = payload_ref[:, part, :] - returned_ref[:, part, :]
+        residual_ref[part] = jnp.where(in_use, difference, 0.0)
+    for ahead in range(1, senders):
+        payload_copy(ahead).wait_send()
+        return_copy(ahead).wait_send()
+    for ahead in range(1, owners):
+        entry_copy(ahead).wait_send()
+        partial_copy(ahead).wait_send()
+    store.wait()
+
+
+def imaging_cycle(payload, slots, live, counts, band, model, threshold, plan, grid_side, owners):
+    senders = payload.shape[0]
     lists, _, cap = slots.shape
-    return pl.pallas_call(
-        functools.partial(gather_kernel, senders, width),
-        out_shape=jax.ShapeDtypeStruct((lists, 8, cap), F32),
-        in_specs=vmem(3),
-        out_specs=vmem(1)[0],
-        scratch_shapes=[pltpu.VMEM((received.shape[1], padded), BF16)],
-        compiler_params=params(),
-        name="gather_entries",
-    )(received, slots, live)
-
-
-def scatter_values(values, slots, live, senders, width):
-    return pl.pallas_call(
-        functools.partial(scatter_kernel, senders, width),
-        out_shape=jax.ShapeDtypeStruct((senders, 2 * LANES), F32),
-        in_specs=vmem(3),
-        out_specs=vmem(1)[0],
-        compiler_params=params(),
-        name="scatter_values",
-    )(values, slots, live)
-
-
-def imaging_cycle(entries, band, model, threshold, plan, grid_side):
-    owners, lists, _, cap = entries.shape
-    row_local, _, _, width, group = plan[:5]
+    _, row_local, _, _, width, group = plan[:6]
     lead = grid_side // LANES
     rows_total = model.shape[0] * group
     steps = owners * lists * (cap // width)
-    tables = transform_tables(grid_side)
+    padded = -(-3 * senders // LANES) * LANES
+    first, second, third, last, twist, twist_t = (
+        jnp.asarray(table) for table in transform_tables(grid_side)
+    )
+    in_vmem = pl.BlockSpec(memory_space=pltpu.VMEM)
+    anywhere = pl.BlockSpec(memory_space=pl.ANY)
     return pl.pallas_call(
         functools.partial(cycle_kernel, plan),
         out_shape=(
             jax.ShapeDtypeStruct(model.shape, F32),
-            jax.ShapeDtypeStruct((owners, lists, 2, cap), F32),
+            jax.ShapeDtypeStruct((2, senders, LANES), F32),
         ),
-        in_specs=vmem(3) + [pl.BlockSpec(memory_space=pltpu.SMEM)] + vmem(6),
-        out_specs=tuple(vmem(2)),
+        in_specs=[in_vmem] * 5
+        + [pl.BlockSpec(memory_space=pltpu.SMEM)]
+        + [in_vmem] * 4
+        + [anywhere] * 3,
+        out_specs=(anywhere, in_vmem),
         scratch_shapes=[
+            pltpu.VMEM(payload.shape, F32),
+            pltpu.VMEM((7 * LANES, padded), BF16),
+            pltpu.VMEM((owners, lists, 8, cap), F32),
+            pltpu.VMEM(first.shape, BF16),
+            pltpu.VMEM(last.shape, BF16),
+            pltpu.VMEM(model.shape, F32),
+            pltpu.VMEM(model.shape, F32),
             pltpu.VMEM((rows_total, 2 * lead, LANES), F32),
             pltpu.VMEM((steps, 2 * row_local, width), F32),
+            pltpu.VMEM((owners, lists, 2, cap), F32),
+            pltpu.VMEM((owners, lists, 2, cap), F32),
+            pltpu.VMEM((senders, 2, LANES), F32),
+            pltpu.VMEM((senders, 2, LANES), F32),
+            pltpu.SemaphoreType.DMA((4,)),
+            pltpu.SemaphoreType.DMA((senders,)),
+            pltpu.SemaphoreType.DMA((senders,)),
+            pltpu.SemaphoreType.DMA((owners,)),
+            pltpu.SemaphoreType.DMA((owners,)),
+            pltpu.SemaphoreType.DMA((owners,)),
+            pltpu.SemaphoreType.DMA((owners,)),
+            pltpu.SemaphoreType.DMA((senders,)),
+            pltpu.SemaphoreType.DMA((senders,)),
         ],
-        compiler_params=params(),
+        compiler_params=pltpu.CompilerParams(
+            vmem_limit_bytes=VMEM_BYTES, collective_id=0, has_side_effects=True
+        ),
         name="imaging_cycle",
-    )(entries, band, model, threshold, *[jnp.asarray(table) for table in tables])
+    )(
+        payload, slots, live, counts, band, threshold,
+        second, third, twist, twist_t, first, last, model,
+    )
 
 
 def per_device(
@@ -404,7 +584,6 @@
     fft_devices = lax.axis_size("fft")
     chan_devices = lax.axis_size("chan")
     senders = fft_devices * chan_devices
-    per_pair = visibilities.shape[3]
     local_tiles = tile_lists.shape[1]
     tile_cap = tile_lists.shape[2]
     chan_local, row_local, grid_side = model_image.shape
@@ -417,14 +596,12 @@
     group = math.gcd(row_local, 8)
 
     labels = jnp.stack([cell_row, cell_column, kernel_class], axis=1).astype(F32)
-    payload = jnp.concatenate([visibilities, positions, labels], axis=1)[0]
-    payload = payload.transpose(1, 0, 2).reshape(senders, 7 * per_pair)
-    received = lax.all_to_all(payload, ("fft", "chan"), split_axis=0, concat_axis=0, tiled=True)
+    blank = jnp.zeros_like(visibilities[:, :1])
+    payload = jnp.concatenate([visibilities, positions, labels, blank], axis=1)[0]
+    payload = payload.transpose(1, 0, 2)
     slots = tile_lists[0][:, None, :]
     live = jnp.arange(tile_cap, dtype=jnp.int32)[None, :] < tile_counts[0][:, None]
     live = live.astype(F32)[:, None, :]
-    entries = gather_entries(received, slots, live, width)
-    entries = lax.all_gather(entries, "fft", axis=0, tiled=False)
 
     band_index = np.arange(facet_rows)[:, None] * (grid_side // 2 + np.arange(BU))[None, :]
     band_cos, band_sin = unit(band_index, facet_rows)
@@ -437,19 +614,24 @@
     rows_total = chan_local * row_local
     model = model_image.reshape(rows_total // group, group, lanes_total, LANES)
     model = model.transpose(0, 2, 1, 3).reshape(rows_total // group, lanes_total * group, LANES)
-    plan = (row_local, tiles_each, tile_cols, width, group, dirty_scale, back_scale)
-    updated, partial = imaging_cycle(entries, band, model, threshold, plan, grid_side)
+    plan = (
+        chan_devices, row_local, tiles_each, tile_cols, width, group, dirty_scale, back_scale
+    )
+    updated, residuals = imaging_cycle(
+        payload,
+        slots,
+        live,
+        send_counts.reshape(senders, 1),
+        band,
+        model,
+        threshold,
+        plan,
+        grid_side,
+        fft_devices,
+    )
     updated = updated.reshape(rows_total // group, lanes_total, group, LANES)
     updated = updated.transpose(0, 2, 1, 3).reshape(model_image.shape)
-
-    partial = lax.all_to_all(partial, "fft", split_axis=0, concat_axis=0, tiled=True)
-    predicted = jnp.sum(partial, axis=0)
-    outgoing = scatter_values(predicted, slots, live, senders, width)
-    returned = lax.all_to_all(outgoing, ("fft", "chan"), split_axis=0, concat_axis=0, tiled=True)
-    returned = returned.reshape(senders, 2, per_pair).transpose(1, 0, 2)[None]
-    sent_live = jnp.arange(per_pair, dtype=jnp.int32)[None, None, :] < send_counts[0][None, :, None]
-    residuals = jnp.where(sent_live[:, None], visibilities - returned, jnp.zeros_like(visibilities))
-    return (updated, residuals)
+    return (updated, residuals[None])
 
 
 def solution(mesh):

time: 171 us -> 128 us (0.75)
  blocking collectives: 45.5 us -> 0 us
  Pallas kernels: 93.4 us -> 113 us
  waiting for transfers between devices: 11.2 us -> 0 us
  starting transfers between devices: 9.82 us -> 0 us
  local copies, waits for them, and re-layouts: 5.53 us -> 10.7 us
    all_gather x1 -> x0, blocking collectives: 34.4 us -> none  [per_device(): entries = lax.all_gather(entries, 'fft', axis=0, tiled=False)]
    pallas_call x1, Pallas kernels: 85.4 us -> 113 us  [imaging_cycle(): pl.pallas_call(functools.partial(cycle_kernel, plan), out_shape=(jax.Shap...]
    all_to_all x2 -> x0, waiting for transfers between devices: 11.2 us -> none  [the longest x1 7.17 us: per_device(): lax.all_to_all(outgoing, ('fft', 'chan'), split_axis=0, concat_axis=0, ti...]
    all_to_all x1 -> x0, blocking collectives: 11.1 us -> none  [per_device(): lax.all_to_all(partial, 'fft', split_axis=0, concat_axis=0, tiled=True)]
    all_to_all x2 -> x0, starting transfers between devices: 9.82 us -> none  [the longest x1 7.3 us: per_device(): lax.all_to_all(payload, ('fft', 'chan'), split_axis=0, concat_axis=0, til...]
    pallas_call x2 -> x0, Pallas kernels: 7.97 us -> none  [the longest x1 4.51 us: gather_entries(): pl.pallas_call(functools.partial(gather_kernel, senders, width), out_shap...]
    unnamed x5 -> x6, local copies, waits for them, and re-layouts: 0.66 us -> 6.67 us
    all_to_all x2 -> x0, local copies, waits for them, and re-layouts: 2.16 us -> none  [the longest x1 1.4 us: per_device(): lax.all_to_all(outgoing, ('fft', 'chan'), split_axis=0, concat_axis=0, ti...]
  transfers between devices with their start and end apart: 2 -> 0, of which waited for: 2 -> 0; matrix products, arithmetic and copies ran while one was open for 2% -> 0% of each run, Pallas kernels for 0% -> 0%
where the time goes in v3:
time: 128 us; the launch traced here: 127 us
  Pallas kernels  113 us (88%)
  local copies, waits for them, and re-layouts  10.7 us (8%)
  other arithmetic  2.86 us (2%)
    pallas_call x1, Pallas kernels, imaging_cycle(): pl.pallas_call(functools.partial(cycle_kernel, plan), out_shape=(jax.Shap...  113 us
    unnamed x6, local copies, waits for them, and re-layouts  6.67 us

profile of v3, /device:TPU:0, one launch (start us, length us, event | category | flops | bytes accessed | tf_op | source)
XLA Modules:
  0.0 127.4 jit_solution(14588353566316097400)
XLA Ops:
  0.6 0.1 pad.3.clone
  0.7 1.3 %broadcast_in_dim_squeeze.4.slot_ref = s32[8,1,384]{2,1,0:T(1,128)} reshape(s32[1,8,384]{2,1,0:T(8,128)} %param.23) | data formatting | bytes 24576 | tf_op jit(solution)/shard_map/broadcast_in_dim;squeeze | solution.py:602
  2.0 1.3 %compare_convert_fusion.live_ref = f32[8,1,384]{2,1,0:T(1,128)} fusion(s32[8]{0:T(128)} %bitcast.29), kind=kLoop, calls=%fused_computation.2 | loop fusion | flops 6144 | bytes 12320 | tf_op jit(solution)/shard_map/convert_element_type | solution.py:604
  3.3 1.3 %dynamic-slice_bitcast_fusion.band_ref = bf16[32,192]{1,0:T(8,128)(2,1)} fusion(bf16[8,32,192]{2,1,0:T(8,128)(2,1)} %constant.28.clone, s32[]{:T(128)S(6)} %select_n.4), kind=kLoop, calls=%fused_computation.3 | loop fusion | bytes 24580 | tf_op jit(solution)/shard_map/jit(dynamic_index_in_dim)/squeeze | solution.py:610
  4.7 1.3 %copy.21.count_ref = s32[32,1]{1,0:T(8,128)} copy(s32[32,1]{0,1:T(1,128)} %bitcast.30) | data formatting | bytes 256 | tf_op jit(solution)/shard_map/reshape | solution.py:624
  6.0 0.8 copy.19
  6.8 0.8 copy.20
  7.6 0.8 add_convert_fusion
  8.4 0.7 maximum_bitcast_fusion.payload_ref
  9.1 113.2 %imaging_cycle.1 = (f32[4,2048,128]{2,1,0:T(8,128)}, f32[2,32,128]{2,1,0:T(8,128)}) custom-call(f32[32,8,128]{2,1,0:T(8,128)} %maximum_bitcast_fusion.payload_ref, s32[8,1,384]{2,1,0:T(1,128)} %broadcast_in_dim_squeeze.4.slot_ref, f32[8,1,384]{2,1,0:T(1,128)} %compare_convert_fusion.live_ref, s32[32,1]{1,0:T(8,128)} %copy.21.count_ref, ...), custom_call_target="tpu_custom_call" | custom-call | tf_op jit(solution)/shard_map/imaging_cycle/pallas_call | solution.py:527
  122.3 0.0 copy-start
  122.3 4.5 %copy.24 = f32[2,16,32768]{2,1,0:T(8,128)} copy(f32[2,16,32768]{2,1,0:T(8,128)} %bitcast.24) | data formatting | bytes 8388608
  126.8 0.0 copy-done
  126.8 0.6 copy.25
Async XLA Ops:
  122.3 4.5 %copy-start = (f32[2,32,128]{2,1,0:T(8,128)S(1)}, f32[2,32,128]{2,1,0:T(8,128)}, u32[]{:S(2)}) copy-start(f32[2,32,128]{2,1,0:T(8,128)} %get-tuple-element.5) | copy-start | bytes 98308

commit v4 on v3

--- a/solution.py
+++ b/solution.py
@@ -200,8 +200,9 @@
     def slots_of(index):
         k = index // pieces
         at = pl.multiple_of(lax.rem(index, pieces) * width, LANES)
-        slots = slot_ref[k, :, pl.ds(at, width)]
-        live = live_ref[k, :, pl.ds(at, width)]
+        slots = slot_ref[pl.ds(k, 1), pl.ds(at, width)]
+        entry = lax.broadcasted_iota(jnp.int32, (1, width), 1) + at
+        live = jnp.where(entry < live_ref[k], 1.0, 0.0)
         source = slots // LANES
         place = slots - source * LANES
         sender = lax.broadcasted_iota(jnp.int32, (senders, width), 0)
@@ -289,7 +290,7 @@
         row_kernel = jnp.where(
             jnp.abs(distance) <= half_width, jnp.exp(offset * offset * rate), 0.0
         )
-        phased = dot(band_ref[...], side3(row_kernel, 0), NN)
+        phased = dot(band_ref[fft_at], side3(row_kernel, 0), NN)
         row_ref[owner * rounds + index] = phased
         phased_re, phased_im = phased[:row_local], phased[row_local:]
         weight_re = entries[0:1] * phased_re - entries[1:2] * phased_im
@@ -337,7 +338,7 @@
             grid_step(owner, index)
             return inner_carry
 
-        lax.fori_loop(0, rounds, step, 0, unroll=2)
+        lax.fori_loop(0, rounds, step, 0, unroll=4)
         return carry
 
     lax.fori_loop(0, owners, grid_owner, 0)
@@ -442,7 +443,7 @@
             degrid_step(owner, index)
             return inner_carry
 
-        lax.fori_loop(0, rounds, step, 0, unroll=2)
+        lax.fori_loop(0, rounds, step, 0, unroll=4)
 
         @pl.when(ahead > 0)
         def _():
@@ -513,7 +514,7 @@
 
 def imaging_cycle(payload, slots, live, counts, band, model, threshold, plan, grid_side, owners):
     senders = payload.shape[0]
-    lists, _, cap = slots.shape
+    lists, cap = slots.shape
     _, row_local, _, _, width, group = plan[:6]
     lead = grid_side // LANES
     rows_total = model.shape[0] * group
@@ -523,6 +524,7 @@
         jnp.asarray(table) for table in transform_tables(grid_side)
     )
     in_vmem = pl.BlockSpec(memory_space=pltpu.VMEM)
+    in_smem = pl.BlockSpec(memory_space=pltpu.SMEM)
     anywhere = pl.BlockSpec(memory_space=pl.ANY)
     return pl.pallas_call(
         functools.partial(cycle_kernel, plan),
@@ -530,8 +532,7 @@
             jax.ShapeDtypeStruct(model.shape, F32),
             jax.ShapeDtypeStruct((2, senders, LANES), F32),
         ),
-        in_specs=[in_vmem] * 5
-        + [pl.BlockSpec(memory_space=pltpu.SMEM)]
+        in_specs=[in_vmem, in_vmem, in_smem, in_vmem, in_vmem, in_smem]
         + [in_vmem] * 4
         + [anywhere] * 3,
         out_specs=(anywhere, in_vmem),
@@ -599,17 +600,10 @@
     blank = jnp.zeros_like(visibilities[:, :1])
     payload = jnp.concatenate([visibilities, positions, labels, blank], axis=1)[0]
     payload = payload.transpose(1, 0, 2)
-    slots = tile_lists[0][:, None, :]
-    live = jnp.arange(tile_cap, dtype=jnp.int32)[None, :] < tile_counts[0][:, None]
-    live = live.astype(F32)[:, None, :]
-
     band_index = np.arange(facet_rows)[:, None] * (grid_side // 2 + np.arange(BU))[None, :]
     band_cos, band_sin = unit(band_index, facet_rows)
     band = np.stack([band_cos, -band_sin]).reshape(2, fft_devices, row_local, BU)
     band = table3(band.transpose(1, 0, 2, 3).reshape(fft_devices, 2 * row_local, BU))
-    band = lax.dynamic_index_in_dim(
-        jnp.asarray(band), lax.axis_index("fft"), axis=0, keepdims=False
-    )
     lanes_total = grid_side // LANES
     rows_total = chan_local * row_local
     model = model_image.reshape(rows_total // group, group, lanes_total, LANES)
@@ -619,10 +613,10 @@
     )
     updated, residuals = imaging_cycle(
         payload,
-        slots,
-        live,
+        tile_lists[0],
+        tile_counts[0],
         send_counts.reshape(senders, 1),
-        band,
+        jnp.asarray(band),
         model,
         threshold,
         plan,

time: 128 us -> 118 us (0.922)
  Pallas kernels: 113 us -> 108 us
  local copies, waits for them, and re-layouts: 10.7 us -> 8.08 us
  other arithmetic: 2.86 us -> 1.54 us
    pallas_call x1, Pallas kernels: 113 us -> 108 us  [imaging_cycle(): pl.pallas_call(functools.partial(cycle_kernel, plan), out_shape=(jax.Shap...]
    convert_element_type x1 -> x0, other arithmetic: 1.33 us -> none  [per_device(): live = live.astype(F32)[:, None, :]]
    squeeze x1 -> x0, local copies, waits for them, and re-layouts: 1.32 us -> none  [per_device(): lax.dynamic_index_in_dim(jnp.asarray(band), lax.axis_index('fft'), axis=0...]
    another operation x1 -> x0, local copies, waits for them, and re-layouts: 1.31 us -> none  [per_device(): slots = tile_lists[0][:, None, :]]
where the time goes in v4:
time: 118 us
  Pallas kernels  108 us (92%)
  local copies, waits for them, and re-layouts  8.08 us (7%)
  other arithmetic  1.54 us (1%)
    pallas_call x1, Pallas kernels, imaging_cycle(): pl.pallas_call(functools.partial(cycle_kernel, plan), out_shape=(jax.Shap...  108 us
    unnamed x6, local copies, waits for them, and re-layouts  6.67 us

profile of v4, /device:TPU:0, one launch (start us, length us, event | category | flops | bytes accessed | tf_op | source)
XLA Modules:
  0.0 118.0 jit_solution(6925892294367205746)
XLA Ops:
  0.6 0.1 pad.3.clone
  0.7 1.3 %copy.21.count_ref = s32[32,1]{1,0:T(8,128)} copy(s32[32,1]{0,1:T(1,128)} %bitcast.30) | data formatting | bytes 256 | tf_op jit(solution)/shard_map/reshape | solution.py:618
  2.0 0.8 copy.19
  2.8 0.8 copy.20
  3.6 0.8 add_convert_fusion
  4.4 0.7 maximum_bitcast_fusion.payload_ref
  5.2 107.7 %imaging_cycle.1 = (f32[4,2048,128]{2,1,0:T(8,128)}, f32[2,32,128]{2,1,0:T(8,128)}) custom-call(f32[32,8,128]{2,1,0:T(8,128)} %maximum_bitcast_fusion.payload_ref, s32[8,384]{1,0:T(8,128)} %bitcast.28, s32[8]{0:T(128)} %bitcast.29, s32[32,1]{1,0:T(8,128)} %copy.21.count_ref, bf16[8,32,192]{2,1,0:T(8,128)(2,1)} %constant.16.clone.band_ref, f32[2]{0:T(128)} %threshold_ref.1, ...), custom_call_target="tpu_custom_call" | custom-call | tf_op jit(solution)/shard_map/imaging_cycle/pallas_call | solution.py:529
  112.9 0.0 copy-start
  112.9 4.5 %copy.24 = f32[2,16,32768]{2,1,0:T(8,128)} copy(f32[2,16,32768]{2,1,0:T(8,128)} %bitcast.23) | data formatting | bytes 8388608
  117.4 0.0 copy-done
  117.4 0.6 copy.25
Async XLA Ops:
  112.9 4.5 %copy-start = (f32[2,32,128]{2,1,0:T(8,128)S(1)}, f32[2,32,128]{2,1,0:T(8,128)}, u32[]{:S(2)}) copy-start(f32[2,32,128]{2,1,0:T(8,128)} %get-tuple-element.5) | copy-start | bytes 98308
